TPU v7x, 32 devices: a whole 2x2x4 slice. The times are simulated.
32 devices in a mesh: tensor: 2 (over x), dp: 4 (over y, core), context: 4 (over z).
Axes of the slice: x: 2, y: 2, z: 4, core: 2. Of those that a mesh axis runs over, the one named last changes fastest.
Arguments:
- tokens: bfloat16 [8, 2048, 1536], P('dp', 'context'), may hold values from -6 to 6
- out_grad: bfloat16 [8, 2048, 1536], P('dp', 'context'), may hold values from -6 to 6
- span_order: int32 [8], replicated, may hold values from 0 to 7, as said below
- query_weight: float32 [1536, 1536], P(('dp', 'context'), 'tensor'), may hold values from -0.15625 to 0.15625
- key_weight: float32 [1536, 768], P(('dp', 'context'), 'tensor'), may hold values from -0.15625 to 0.15625
- value_projection: float32 [1536, 768], P(('dp', 'context'), 'tensor'), may hold values from -0.15625 to 0.15625
- output_weight: float32 [1536, 1536], P('tensor', ('dp', 'context')), may hold values from -2.5 to 2.5
- gate_weight: float32 [1536, 4096], P(('dp', 'context'), 'tensor'), may hold values from -0.15625 to 0.15625
- up_weight: float32 [1536, 4096], P(('dp', 'context'), 'tensor'), may hold values from -0.15625 to 0.15625
- down_weight: float32 [4096, 1536], P('tensor', ('dp', 'context')), may hold values from -0.09375 to 0.09375
- attention_gain: float32 [1536], P(('dp', 'context')), may hold values from 0.5 to 1.5
- feedforward_gain: float32 [1536], P(('dp', 'context')), may hold values from 0.5 to 1.5
- query_weight_first: float32 [1536, 1536], P(('dp', 'context'), 'tensor'), may hold values from -48 to 48
- key_projection_first_moment: float32 [1536, 768], P(('dp', 'context'), 'tensor'), may hold values from -64 to 64
- value_projection_first_moment: float32 [1536, 768], P(('dp', 'context'), 'tensor'), may hold values from -64 to 64
- output_weight_first: float32 [1536, 1536], P('tensor', ('dp', 'context')), may hold values from -6 to 6
- gate_weight_first: float32 [1536, 4096], P(('dp', 'context'), 'tensor'), may hold values from -28 to 28
- up_weight_first: float32 [1536, 4096], P(('dp', 'context'), 'tensor'), may hold values from -28 to 28
- down_weight_first: float32 [4096, 1536], P('tensor', ('dp', 'context')), may hold values from -48 to 48
- attention_gain_first: float32 [1536], P(('dp', 'context')), may hold values from -80 to 80
- feedforward_gain_first: float32 [1536], P(('dp', 'context')), may hold values from -80 to 80
- query_weight_second: float32 [1536, 1536], P(('dp', 'context'), 'tensor'), may hold values from 180.224 to 1179.648
- key_projection_second_moment: float32 [1536, 768], P(('dp', 'context'), 'tensor'), may hold values from 360.448 to 2359.296
- value_projection_second_moment: float32 [1536, 768], P(('dp', 'context'), 'tensor'), may hold values from 360.448 to 2359.296
- output_weight_second: float32 [1536, 1536], P('tensor', ('dp', 'context')), may hold values from 0.696 to 4.64
- gate_weight_second: float32 [1536, 4096], P(('dp', 'context'), 'tensor'), may hold values from 67.584 to 442.368
- up_weight_second: float32 [1536, 4096], P(('dp', 'context'), 'tensor'), may hold values from 67.584 to 442.368
- down_weight_second: float32 [4096, 1536], P('tensor', ('dp', 'context')), may hold values from 180.224 to 1179.648
- attention_gain_second: float32 [1536], P(('dp', 'context')), may hold values from 491.52 to 3276.8
- feedforward_gain_second: float32 [1536], P(('dp', 'context')), may hold values from 491.52 to 3276.8
Outputs:
- output: float32 [8, 2048, 1536], P('dp', 'context')
- input_grad: float32 [8, 2048, 1536], P('dp', 'context')
- query_weight_gradient: float32 [1536, 1536], P(('dp', 'context'), 'tensor')
- key_weight_gradient: float32 [1536, 768], P(('dp', 'context'), 'tensor')
- value_weight_gradient: float32 [1536, 768], P(('dp', 'context'), 'tensor')
- output_weight_gradient: float32 [1536, 1536], P('tensor', ('dp', 'context'))
- gate_weight_gradient: float32 [1536, 4096], P(('dp', 'context'), 'tensor')
- up_weight_gradient: float32 [1536, 4096], P(('dp', 'context'), 'tensor')
- down_weight_gradient: float32 [4096, 1536], P('tensor', ('dp', 'context'))
- attention_gain_gradient: float32 [1536], P(('dp', 'context'))
- feedforward_gain_gradient: float32 [1536], P(('dp', 'context'))
- query_weight_updated: float32 [1536, 1536], P(('dp', 'context'), 'tensor')
- key_weight_updated: float32 [1536, 768], P(('dp', 'context'), 'tensor')
- value_weight_updated: float32 [1536, 768], P(('dp', 'context'), 'tensor')
- output_weight_updated: float32 [1536, 1536], P('tensor', ('dp', 'context'))
- gate_weight_updated: float32 [1536, 4096], P(('dp', 'context'), 'tensor')
- up_weight_updated: float32 [1536, 4096], P(('dp', 'context'), 'tensor')
- down_weight_updated: float32 [4096, 1536], P('tensor', ('dp', 'context'))
- attention_gain_updated: float32 [1536], P(('dp', 'context'))
- feedforward_gain_updated: float32 [1536], P(('dp', 'context'))
- query_weight_first_updated: float32 [1536, 1536], P(('dp', 'context'), 'tensor')
- key_weight_first_updated: float32 [1536, 768], P(('dp', 'context'), 'tensor')
- value_weight_first_updated: float32 [1536, 768], P(('dp', 'context'), 'tensor')
- output_weight_first_updated: float32 [1536, 1536], P('tensor', ('dp', 'context'))
- gate_weight_first_updated: float32 [1536, 4096], P(('dp', 'context'), 'tensor')
- up_weight_first_updated: float32 [1536, 4096], P(('dp', 'context'), 'tensor')
- down_weight_first_updated: float32 [4096, 1536], P('tensor', ('dp', 'context'))
- attention_gain_first_updated: float32 [1536], P(('dp', 'context'))
- feedforward_gain_first_updated: float32 [1536], P(('dp', 'context'))
- query_weight_second_updated: float32 [1536, 1536], P(('dp', 'context'), 'tensor')
- key_weight_second_updated: float32 [1536, 768], P(('dp', 'context'), 'tensor')
- value_weight_second_updated: float32 [1536, 768], P(('dp', 'context'), 'tensor')
- output_weight_second_updated: float32 [1536, 1536], P('tensor', ('dp', 'context'))
- gate_weight_second_updated: float32 [1536, 4096], P(('dp', 'context'), 'tensor')
- up_weight_second_updated: float32 [1536, 4096], P(('dp', 'context'), 'tensor')
- down_weight_second_updated: float32 [4096, 1536], P('tensor', ('dp', 'context'))
- attention_gain_second_updated: float32 [1536], P(('dp', 'context'))
- feedforward_gain_second_updated: float32 [1536], P(('dp', 'context'))
Inputs may be any that keep to these rules, and one draw needn't show every extreme that they name: `span_order`: a permutation of 0 to 7 in which the spans of slots 2 c and 2 c + 1 add up to 7.
All inputs are finite; a program needn't handle non-finite values.
Results may differ from a plain program's by a relative error of at most 0.035.
Values may be sent and summed in bfloat16 or wider, within the bound.
No kernel may reach another device: no remote copies, remote signals or barrier semaphores. Data moves between devices by JAX's collectives and lax.ppermute only.
A program may use at most 320 MiB of HBM per device.

v0:
```python
import functools
import math

import jax
import jax.numpy as jnp
from jax import lax
from jax.experimental import pallas as pl
from jax.experimental.pallas import tpu as pltpu
from jax.sharding import PartitionSpec as P

MODEL_DIMENSION = 1536
QUERY_HEADS = 16
KEY_VALUE_HEADS = 8
HEAD_DIMENSION = 96
FF_TILE = 512
GRAD_TILE = 1024
SMALL = pl.CostEstimate(flops=1000, bytes_accessed=1000, transcendentals=0)
LARGE = pl.CostEstimate(flops=10**12, bytes_accessed=1000, transcendentals=0)
DP, CX, TP = "dp", "context", "tensor"


norm_eps = 1e-05
rope_base = 100000.0
beta_one = 0.9
beta_two = 0.95
adam_eps = 1e-08
gain_rate = 0.6
decay_rate = 0.1
step_count = 4.0


HD = HEAD_DIMENSION
HALF = 48
LOG2E = 1.4426950408889634
f32 = jnp.float32
bf16 = jnp.bfloat16

def nn(a, b):
    return lax.dot_general(a, b, (((1,), (0,)), ((), ())), preferred_element_type=f32)

def nt(a, b):
    return lax.dot_general(a, b, (((1,), (1,)), ((), ())), preferred_element_type=f32)

def spread_heads(kv_refs, k_heads, kv_heads, rows, base):
    for s, ref in enumerate(kv_refs):
        for h in range(kv_heads):
            k_heads[h, s * rows:(s + 1) * rows, :] = ref[:, base + h * HD: base + (h + 1) * HD]

def forward_kernel(kv_heads, group, span_rows, spans, qt, *refs):
    blocks = len(refs) - 3 - 6
    kv_refs = refs[:blocks]
    out_low, out_t, log_total = refs[blocks:blocks + 3]
    k_heads, v_t, q_wide, top, total, acc = refs[blocks + 3:]
    rows = kv_refs[0].shape[0]
    kv_width = kv_heads * HD
    wide = group * span_rows
    scale = LOG2E / math.sqrt(HD)
    spread_heads(kv_refs, k_heads, kv_heads, rows, 0)
    for s, ref in enumerate(kv_refs):
        v_t[:, s * rows:(s + 1) * rows] = ref[:, kv_width:].T
    for h in range(kv_heads):
        for i in range(2):
            q_wide[h, i] = jnp.concatenate(
                [qt[(h * group + n) * HD:(h * group + n + 1) * HD, i * span_rows:(i + 1) * span_rows]
                 for n in range(group)], axis=1)
    key_at = lax.broadcasted_iota(jnp.int32, (span_rows, wide), 0)
    query_at = lax.broadcasted_iota(jnp.int32, (span_rows, wide), 1) % span_rows
    keep = key_at <= query_at
    for i in range(2):
        for h in range(kv_heads):
            scores = nn(k_heads[h, i * span_rows:(i + 1) * span_rows, :], q_wide[h, i]) * scale
            scores = jnp.where(keep, scores, -1e30)
            peak = jnp.max(scores, axis=0, keepdims=True)
            probs = jnp.exp2(scores - peak)
            top[h, i] = peak
            total[h, i] = jnp.sum(probs, axis=0, keepdims=True)
            acc[h, i] = nn(v_t[h * HD:(h + 1) * HD, i * span_rows:(i + 1) * span_rows], probs.astype(bf16))

    def visit(j, _):
        start = pl.multiple_of(j * span_rows, span_rows)
        for i in range(2):
            @pl.when(spans[2 + j] < spans[i])
            def _():
                for h in range(kv_heads):
                    scores = nn(k_heads[h, pl.ds(start, span_rows), :], q_wide[h, i]) * scale
                    before = top[h, i]
                    peak = jnp.maximum(before, jnp.max(scores, axis=0, keepdims=True))
                    fade = jnp.exp2(before - peak)
                    probs = jnp.exp2(scores - peak)
                    top[h, i] = peak
                    total[h, i] = total[h, i] * fade + jnp.sum(probs, axis=0, keepdims=True)
                    acc[h, i] = acc[h, i] * fade + nn(
                        v_t[h * HD:(h + 1) * HD, pl.ds(start, span_rows)], probs.astype(bf16))
        return 0
    lax.fori_loop(0, 2 * blocks, visit, 0)
    for i in range(2):
        cols = slice(i * span_rows, (i + 1) * span_rows)
        for h in range(kv_heads):
            sums = total[h, i]
            whole = (acc[h, i] / sums).astype(bf16)
            level = top[h, i] + jnp.log2(sums)
            for n in range(group):
                at = h * group + n
                lanes = slice(n * span_rows, (n + 1) * span_rows)
                out_t[at * HD:(at + 1) * HD, cols] = whole[:, lanes]
                log_total[at:at + 1, cols] = level[:, lanes]
    out_low[...] = out_t[...].T

def attention_forward(spans, qt, kv_blocks):
    width, rows = qt.shape
    kv_heads = kv_blocks[0].shape[1] // (2 * HD)
    heads = width // HD
    group = heads // kv_heads
    span_rows = rows // 2
    keys = rows * len(kv_blocks)
    wide = group * span_rows
    whole = lambda: pl.BlockSpec(memory_space=pltpu.VMEM)
    return pl.pallas_call(
        functools.partial(forward_kernel, kv_heads, group, span_rows),
        in_specs=[pl.BlockSpec(memory_space=pltpu.SMEM)] + [whole() for _ in range(1 + len(kv_blocks))],
        out_specs=[whole(), whole(), whole()],
        out_shape=[jax.ShapeDtypeStruct((rows, width), bf16), jax.ShapeDtypeStruct((width, rows), bf16),
                   jax.ShapeDtypeStruct((heads, rows), f32)],
        scratch_shapes=[pltpu.VMEM((kv_heads, keys, HD), bf16), pltpu.VMEM((kv_heads * HD, keys), bf16),
                        pltpu.VMEM((kv_heads, 2, HD, wide), bf16), pltpu.VMEM((kv_heads, 2, 1, wide), f32),
                        pltpu.VMEM((kv_heads, 2, 1, wide), f32), pltpu.VMEM((kv_heads, 2, HD, wide), f32)],
        compiler_params=pltpu.CompilerParams(vmem_limit_bytes=48 * 1024 * 1024),
        cost_estimate=SMALL,
        name="attention_forward",
    )(spans, qt, *kv_blocks)

def backward_kernel(kv_heads, group, span_rows, blocks, spans, qt, dot_, out_t, log_total, cos_t, sin_t, *refs):
    kv_refs = refs[:blocks]
    dq_low, kept, sent = refs[blocks:blocks + 3]
    k_heads, v_heads, k_t, q_wide, d_wide, level, inner, dq_acc, dk_acc, dv_acc = refs[blocks + 3:]
    rows = kv_refs[0].shape[0]
    kv_width = kv_heads * HD
    wide = group * span_rows
    scale = 1.0 / math.sqrt(HD)
    spread_heads(kv_refs, k_heads, kv_heads, rows, 0)
    spread_heads(kv_refs, v_heads, kv_heads, rows, kv_width)
    for s, ref in enumerate(kv_refs):
        k_t[:, s * rows:(s + 1) * rows] = ref[:, :kv_width].T
    for h in range(kv_heads):
        for i in range(2):
            cols = slice(i * span_rows, (i + 1) * span_rows)
            heads = [slice((h * group + n) * HD, (h * group + n + 1) * HD) for n in range(group)]
            q_wide[h, i] = jnp.concatenate([qt[at, cols] for at in heads], axis=1)
            d_wide[h, i] = jnp.concatenate([dot_[at, cols] for at in heads], axis=1)
            level[h, i] = jnp.concatenate([log_total[h * group + n:h * group + n + 1, cols] for n in range(group)], axis=1)
            inner[h, i] = jnp.concatenate(
                [jnp.sum(dot_[at, cols].astype(f32) * out_t[at, cols].astype(f32), axis=0, keepdims=True) for at in heads], axis=1)
    dk_acc[...] = jnp.zeros_like(dk_acc)
    dv_acc[...] = jnp.zeros_like(dv_acc)
    key_at = lax.broadcasted_iota(jnp.int32, (span_rows, wide), 0)
    query_at = lax.broadcasted_iota(jnp.int32, (span_rows, wide), 1) % span_rows
    keep = key_at <= query_at

    def pair(h, i, at, masked):
        scores = nn(k_heads[h, at, :], q_wide[h, i]) * (scale * LOG2E)
        probs = jnp.exp2(scores - level[h, i])
        if masked:
            probs = jnp.where(keep, probs, 0.0)
        dprobs = nn(v_heads[h, at, :], d_wide[h, i])
        dscores = (probs * (dprobs - inner[h, i])).astype(bf16)
        head = slice(h * HD, (h + 1) * HD)
        dv_acc[head, at] += nt(d_wide[h, i], probs.astype(bf16))
        dk_acc[head, at] += nt(q_wide[h, i], dscores)
        step = nn(k_t[head, at], dscores)
        if masked:
            dq_acc[h, i] = step
        else:
            dq_acc[h, i] += step

    for i in range(2):
        for h in range(kv_heads):
            pair(h, i, slice(i * span_rows, (i + 1) * span_rows), True)

    def visit(j, _):
        start = pl.multiple_of(j * span_rows, span_rows)
        for i in range(2):
            @pl.when(spans[2 + j] < spans[i])
            def _():
                for h in range(kv_heads):
                    pair(h, i, pl.ds(start, span_rows), False)
        return 0
    lax.fori_loop(0, 2 * blocks, visit, 0)
    for i in range(2):
        cols = slice(i * span_rows, (i + 1) * span_rows)
        cos_part, sin_part = cos_t[:, cols], sin_t[:, cols]
        parts = []
        for h in range(kv_heads):
            for n in range(group):
                grad = dq_acc[h, i, :, n * span_rows:(n + 1) * span_rows] * scale
                lead, trail = grad[:HALF], grad[HALF:]
                parts += [(lead * cos_part + trail * sin_part).astype(bf16), (trail * cos_part - lead * sin_part).astype(bf16)]
        dq_low[cols, :] = jnp.concatenate(parts, axis=0).T
    for s in range(blocks):
        cols = slice(s * rows, (s + 1) * rows)
        ref = (kept, sent)[s % 2]
        ref[s // 2, :kv_width, :] = (dk_acc[:, cols] * scale).astype(bf16)
        ref[s // 2, kv_width:, :] = dv_acc[:, cols].astype(bf16)

def attention_backward(dot_, spans, qt, out_t, log_total, cos_t, sin_t, kv_blocks):
    width, rows = qt.shape
    kv_heads = kv_blocks[0].shape[1] // (2 * HD)
    heads = width // HD
    group = heads // kv_heads
    span_rows = rows // 2
    blocks = len(kv_blocks)
    keys = rows * blocks
    wide = group * span_rows
    kv_width = kv_heads * HD
    whole = lambda: pl.BlockSpec(memory_space=pltpu.VMEM)
    return pl.pallas_call(
        functools.partial(backward_kernel, kv_heads, group, span_rows, blocks),
        in_specs=[pl.BlockSpec(memory_space=pltpu.SMEM)] + [whole() for _ in range(6 + blocks)],
        out_specs=[whole() for _ in range(3)],
        out_shape=[jax.ShapeDtypeStruct((rows, width), bf16)] + [jax.ShapeDtypeStruct((blocks // 2, 2 * kv_width, rows), bf16)] * 2,
        scratch_shapes=[pltpu.VMEM((kv_heads, keys, HD), bf16), pltpu.VMEM((kv_heads, keys, HD), bf16),
                        pltpu.VMEM((kv_width, keys), bf16),
                        pltpu.VMEM((kv_heads, 2, HD, wide), bf16), pltpu.VMEM((kv_heads, 2, HD, wide), bf16),
                        pltpu.VMEM((kv_heads, 2, 1, wide), f32), pltpu.VMEM((kv_heads, 2, 1, wide), f32),
                        pltpu.VMEM((kv_heads, 2, HD, wide), f32),
                        pltpu.VMEM((kv_width, keys), f32), pltpu.VMEM((kv_width, keys), f32)],
        compiler_params=pltpu.CompilerParams(vmem_limit_bytes=56 * 1024 * 1024),
        cost_estimate=LARGE,
        name="attention_backward",
    )(spans, qt, dot_, out_t, log_total, cos_t, sin_t, *kv_blocks)

def project_kernel(q_width, kv_width, x, gain, w, cos_t, sin_t, n1, qt, kv):
    values = x[...].astype(f32)
    inverse = lax.rsqrt(jnp.mean(values * values, axis=-1, keepdims=True) + 1e-05)
    normed = (values * inverse * gain[...]).astype(bf16)
    n1[...] = normed
    both = nn(normed, w[:, :q_width + kv_width])
    rows = both.shape[0]
    turned = both.T
    cos_part, sin_part = cos_t[...], sin_t[...]
    parts = []
    for h in range((q_width + kv_width) // HD):
        lead = turned[h * HD:h * HD + HALF]
        trail = turned[h * HD + HALF:(h + 1) * HD]
        parts += [(lead * cos_part - trail * sin_part).astype(bf16), (trail * cos_part + lead * sin_part).astype(bf16)]
    cut = q_width // HALF
    qt[...] = jnp.concatenate(parts[:cut], axis=0)
    kv[:, :kv_width] = jnp.concatenate(parts[cut:], axis=0).T
    kv[:, kv_width:] = nn(normed, w[:, q_width + kv_width:q_width + 2 * kv_width]).astype(bf16)

def project(x, gain, w, cos_t, sin_t, q_width, kv_width):
    rows, model = x.shape
    tile = 256
    return pl.pallas_call(
        functools.partial(project_kernel, q_width, kv_width),
        grid=(rows // tile,),
        in_specs=[pl.BlockSpec((tile, model), lambda r: (r, 0)),
                  pl.BlockSpec((1, model), lambda r: (0, 0)),
                  pl.BlockSpec((model, w.shape[1]), lambda r: (0, 0)),
                  pl.BlockSpec((HALF, tile), lambda r: (0, r)),
                  pl.BlockSpec((HALF, tile), lambda r: (0, r))],
        out_specs=[pl.BlockSpec((tile, model), lambda r: (r, 0)),
                   pl.BlockSpec((q_width, tile), lambda r: (0, r)),
                   pl.BlockSpec((tile, 2 * kv_width), lambda r: (r, 0))],
        out_shape=[jax.ShapeDtypeStruct((rows, model), bf16), jax.ShapeDtypeStruct((q_width, rows), bf16),
                   jax.ShapeDtypeStruct((rows, 2 * kv_width), bf16)],
        compiler_params=pltpu.CompilerParams(vmem_limit_bytes=48 * 1024 * 1024),
        cost_estimate=SMALL,
        name="project_heads",
    )(x, gain, w, cos_t, sin_t)


def rotate(values, cosine, sine_part):
    halfway = values.shape[-1] // 2
    leading = values[..., :halfway]
    trailing = values[..., halfway:]
    return jnp.concatenate(
        [leading * cosine - trailing * sine_part, trailing * cosine + leading * sine_part], axis=-1
    )


def rotate_back(values, cosine, sine_part):
    halfway = values.shape[-1] // 2
    leading = values[..., :halfway]
    trailing = values[..., halfway:]
    return jnp.concatenate(
        [leading * cosine + trailing * sine_part, trailing * cosine - leading * sine_part], axis=-1
    )


def norm_back(values, inverse, gain, upstream):
    scaled = gain * upstream
    unit_rows = values * inverse
    result = inverse * (scaled - unit_rows * jnp.mean(scaled * unit_rows, axis=-1, keepdims=True))
    return (result, jnp.sum(upstream * unit_rows, axis=0))


def contract_rows(left_side, right_side):
    return lax.dot_general(
        left_side, right_side, (((0,), (0,)), ((), ())), preferred_element_type=jnp.float32
    )


def contract_cols(left_side, right_side):
    return lax.dot_general(
        left_side, right_side, (((1,), (1,)), ((), ())), preferred_element_type=jnp.float32
    )


def adamw_update(weight, gradient, moment_one, moment_two, rate_value, decay_value):
    first_new = beta_one * moment_one + (1.0 - beta_one) * gradient
    second_new = beta_two * moment_two + (1.0 - beta_two) * gradient * gradient
    corrected = (
        first_new
        / (1.0 - beta_one**step_count)
        / (jnp.sqrt(second_new / (1.0 - beta_two**step_count)) + adam_eps)
    )
    return (weight - rate_value * (corrected + decay_value * weight), first_new, second_new)


def plain_body(
    tokens,
    out_grad,
    span_order,
    query_weight,
    key_weight,
    value_projection,
    output_weight,
    gate_weight,
    up_weight,
    down_weight,
    attention_gain,
    feedforward_gain,
    query_weight_first,
    key_projection_first_moment,
    value_projection_first_moment,
    output_weight_first,
    gate_weight_first,
    up_weight_first,
    down_weight_first,
    attention_gain_first,
    feedforward_gain_first,
    query_weight_second,
    key_projection_second_moment,
    value_projection_second_moment,
    output_weight_second,
    gate_weight_second,
    up_weight_second,
    down_weight_second,
    attention_gain_second,
    feedforward_gain_second,
):
    bf16 = jnp.bfloat16
    f32 = jnp.float32
    gathered = (
        lax.all_gather(query_weight.astype(bf16), (DP, CX), axis=0, tiled=True),
        lax.all_gather(key_weight.astype(bf16), (DP, CX), axis=0, tiled=True),
        lax.all_gather(value_projection.astype(bf16), (DP, CX), axis=0, tiled=True),
        lax.all_gather(output_weight.astype(bf16), (DP, CX), axis=1, tiled=True),
        lax.all_gather(gate_weight.astype(bf16), (DP, CX), axis=0, tiled=True),
        lax.all_gather(up_weight.astype(bf16), (DP, CX), axis=0, tiled=True),
        lax.all_gather(down_weight.astype(bf16), (DP, CX), axis=1, tiled=True),
        lax.all_gather(attention_gain.astype(bf16), (DP, CX), axis=0, tiled=True),
        lax.all_gather(feedforward_gain.astype(bf16), (DP, CX), axis=0, tiled=True),
    )
    (
        query_matrix,
        projected_keys,
        projected_values,
        output_matrix,
        gate_matrix,
        up_matrix,
        down_matrix,
        mixer_gain,
        forward_gain,
    ) = gathered
    sequence_count, sequence_rows, model_width = tokens.shape
    token_count = sequence_count * sequence_rows
    tensor_size = lax.axis_size(TP)
    own_rows = token_count // tensor_size
    span_rows = sequence_rows // 2
    span_total = span_order.shape[0]
    full_rows = span_total * span_rows
    local_heads = query_matrix.shape[1] // HEAD_DIMENSION
    kv_heads = projected_keys.shape[1] // HEAD_DIMENSION
    query_group_width = local_heads // kv_heads
    score_scale = 1.0 / math.sqrt(HEAD_DIMENSION)
    all_positions = (
        span_order[:, None] * span_rows + jnp.arange(span_rows, dtype=jnp.int32)[None, :]
    ).reshape(full_rows)
    context_index = lax.axis_index(CX)
    query_positions = lax.dynamic_slice_in_dim(
        all_positions, context_index * sequence_rows, sequence_rows
    )
    frequency = rope_base ** (-(jnp.arange(HEAD_DIMENSION // 2, dtype=f32) * 2.0) / HEAD_DIMENSION)
    angles = query_positions.astype(f32)[:, None] * frequency[None, :]
    cosine = jnp.cos(angles)[:, None, :]
    sine_part = jnp.sin(angles)[:, None, :]
    stream_in = tokens.astype(f32).reshape(token_count, model_width)
    inverse_one = lax.rsqrt(jnp.mean(stream_in * stream_in, axis=-1, keepdims=True) + norm_eps)
    mixer_scale = mixer_gain.astype(f32)
    first_normalized = (stream_in * inverse_one * mixer_scale).astype(bf16)
    query_raw = jnp.dot(first_normalized, query_matrix, preferred_element_type=f32).reshape(
        sequence_count, sequence_rows, local_heads, HEAD_DIMENSION
    )
    query_vectors = (
        rotate(query_raw, cosine, sine_part)
        .astype(bf16)
        .reshape(sequence_count, sequence_rows, kv_heads, query_group_width, HEAD_DIMENSION)
        .transpose(0, 2, 3, 1, 4)
    )
    unrotated_keys = jnp.dot(first_normalized, projected_keys, preferred_element_type=f32).reshape(
        sequence_count, sequence_rows, kv_heads, HEAD_DIMENSION
    )
    key_rows = (
        rotate(unrotated_keys, cosine, sine_part)
        .astype(bf16)
        .reshape(sequence_count, sequence_rows, kv_heads * HEAD_DIMENSION)
    )
    value_row_slice = (
        jnp.dot(first_normalized, projected_values, preferred_element_type=f32)
        .astype(bf16)
        .reshape(sequence_count, sequence_rows, kv_heads * HEAD_DIMENSION)
    )
    pieces = (
        lax.all_gather(key_rows, CX, axis=1, tiled=True),
        lax.all_gather(value_row_slice, CX, axis=1, tiled=True),
    )
    row_max = jnp.full((sequence_count, kv_heads, query_group_width, sequence_rows), -1e30, f32)
    piece_rows = pieces[0].shape[1]
    key_grid = pieces[0].reshape(sequence_count, piece_rows, kv_heads, HEAD_DIMENSION)
    value_grid = pieces[1].reshape(sequence_count, piece_rows, kv_heads, HEAD_DIMENSION)
    scores = (
        jnp.einsum("shgqd,skhd->shgqk", query_vectors, key_grid, preferred_element_type=f32)
        * score_scale
    )
    allowed = all_positions[None, :] <= query_positions[:, None]
    new_max = jnp.maximum(row_max, jnp.max(jnp.where(allowed, scores, -1e30), axis=-1))
    weights = jnp.where(allowed, jnp.exp(scores - new_max[..., None]), 0.0)
    row_total = jnp.sum(weights, axis=-1)
    summed = jnp.einsum(
        "shgqk,skhd->shgqd", weights.astype(bf16), value_grid, preferred_element_type=f32
    )
    row_max, row_total, summed = (new_max, row_total, summed)
    attention_out = summed / row_total[..., None]
    attention_low = (
        attention_out.transpose(0, 3, 1, 2, 4)
        .reshape(token_count, local_heads * HEAD_DIMENSION)
        .astype(bf16)
    )
    mixed_own = lax.psum_scatter(
        jnp.dot(attention_low, output_matrix, preferred_element_type=f32).astype(jnp.bfloat16),
        TP,
        scatter_dimension=0,
        tiled=True,
    ).astype(jnp.float32)
    tensor_index = lax.axis_index(TP)
    stream_own = (
        lax.dynamic_slice_in_dim(stream_in, tensor_index * own_rows, own_rows, 0) + mixed_own
    )
    stream_mid = lax.all_gather(
        stream_own.astype(jnp.bfloat16), TP, axis=0, tiled=True
    ).astype(stream_own.dtype)
    inverse_two = lax.rsqrt(jnp.mean(stream_mid * stream_mid, axis=-1, keepdims=True) + norm_eps)
    forward_scale = forward_gain.astype(f32)
    normed_two = (stream_mid * inverse_two * forward_scale).astype(bf16)
    gate_float = (
        jnp.dot(normed_two, gate_matrix, preferred_element_type=f32).astype(bf16).astype(f32)
    )
    up_float = jnp.dot(normed_two, up_matrix, preferred_element_type=f32).astype(bf16).astype(f32)
    sigmoid = jax.nn.sigmoid(gate_float)
    hidden = (gate_float * sigmoid * up_float).astype(bf16)
    feed_terms = jnp.dot(hidden, down_matrix, preferred_element_type=f32)
    feed_sum = lax.psum(feed_terms.astype(jnp.bfloat16), TP).astype(jnp.float32)
    output_field = (stream_mid + feed_sum).reshape(sequence_count, sequence_rows, model_width)
    upstream = out_grad.reshape(token_count, model_width)
    hidden_grad = contract_cols(upstream, down_matrix)
    down_grad = contract_rows(hidden, upstream)
    gate_grad_low = (
        hidden_grad * up_float * sigmoid * (1.0 + gate_float * (1.0 - sigmoid))
    ).astype(bf16)
    up_grad_low = (hidden_grad * gate_float * sigmoid).astype(bf16)
    gate_grad = contract_rows(normed_two, gate_grad_low)
    up_grad = contract_rows(normed_two, up_grad_low)
    normed_two_grad = lax.psum_scatter(
        (contract_cols(gate_grad_low, gate_matrix) + contract_cols(up_grad_low, up_matrix)).astype(
            jnp.bfloat16
        ),
        TP,
        scatter_dimension=0,
        tiled=True,
    ).astype(jnp.float32)
    inverse_own = lax.dynamic_slice_in_dim(inverse_two, tensor_index * own_rows, own_rows, 0)
    stream_back, forward_gain_part = norm_back(
        stream_own, inverse_own, forward_scale, normed_two_grad
    )
    stream_grad_own = (
        lax.dynamic_slice_in_dim(upstream, tensor_index * own_rows, own_rows, 0).astype(f32)
        + stream_back
    )
    stream_grad = lax.all_gather(
        stream_grad_own.astype(jnp.bfloat16), TP, axis=0, tiled=True
    ).astype(stream_grad_own.dtype)
    stream_grad_low = stream_grad.astype(bf16)
    output_grad = contract_rows(attention_low, stream_grad_low)
    attention_grad = contract_cols(stream_grad_low, output_matrix)
    head_grad = attention_grad.reshape(
        sequence_count, sequence_rows, kv_heads, query_group_width, HEAD_DIMENSION
    ).transpose(0, 2, 3, 1, 4)
    key_again, value_again = (
        lax.all_gather(key_rows, CX, axis=1, tiled=True),
        lax.all_gather(value_row_slice, CX, axis=1, tiled=True),
    )

    def sequence_back(element):
        query_seq, key_seq, value_seq, max_seq, total_seq, out_seq, grad_seq = element
        key_grid = key_seq.reshape(full_rows, kv_heads, HEAD_DIMENSION)
        value_grid = value_seq.reshape(full_rows, kv_heads, HEAD_DIMENSION)
        accum_grad = (grad_seq / total_seq[..., None]).astype(bf16)
        row_term = jnp.sum(grad_seq * out_seq, axis=-1) / total_seq
        scores = (
            jnp.einsum("hgqd,khd->hgqk", query_seq, key_grid, preferred_element_type=f32)
            * score_scale
        )
        allowed = all_positions[None, :] <= query_positions[:, None]
        weights = jnp.where(allowed, jnp.exp(scores - max_seq[..., None]), 0.0)
        value_dot = jnp.einsum("hgqd,khd->hgqk", accum_grad, value_grid, preferred_element_type=f32)
        score_grad = (weights * (value_dot - row_term[..., None])).astype(bf16)
        query_part = (
            jnp.einsum("hgqk,khd->hgqd", score_grad, key_grid, preferred_element_type=f32)
            * score_scale
        )
        key_part = (
            jnp.einsum("hgqk,hgqd->khd", score_grad, query_seq, preferred_element_type=f32)
            * score_scale
        )
        value_part = jnp.einsum(
            "hgqk,hgqd->khd", weights.astype(bf16), accum_grad, preferred_element_type=f32
        )
        return (
            query_part,
            key_part.reshape(full_rows, kv_heads * HEAD_DIMENSION),
            value_part.reshape(full_rows, kv_heads * HEAD_DIMENSION),
        )

    query_grads, key_grads, value_grads = lax.map(
        sequence_back,
        (query_vectors, key_again, value_again, row_max, row_total, attention_out, head_grad),
    )
    key_shards, value_shards = (
        lax.psum_scatter(
            key_grads.astype(jnp.bfloat16), CX, scatter_dimension=1, tiled=True
        ).astype(jnp.float32),
        lax.psum_scatter(
            value_grads.astype(jnp.bfloat16), CX, scatter_dimension=1, tiled=True
        ).astype(jnp.float32),
    )
    query_back = (
        rotate_back(
            query_grads.transpose(0, 3, 1, 2, 4).reshape(
                sequence_count, sequence_rows, local_heads, HEAD_DIMENSION
            ),
            cosine,
            sine_part,
        )
        .reshape(token_count, local_heads * HEAD_DIMENSION)
        .astype(bf16)
    )
    key_back = (
        rotate_back(
            key_shards.reshape(sequence_count, sequence_rows, kv_heads, HEAD_DIMENSION),
            cosine,
            sine_part,
        )
        .reshape(token_count, kv_heads * HEAD_DIMENSION)
        .astype(bf16)
    )
    value_back = value_shards.reshape(token_count, kv_heads * HEAD_DIMENSION).astype(bf16)
    query_wgrad = contract_rows(first_normalized, query_back)
    key_wgrad = contract_rows(first_normalized, key_back)
    value_wgrad = contract_rows(first_normalized, value_back)
    normed_one_part = (
        contract_cols(query_back, query_matrix)
        + contract_cols(key_back, projected_keys)
        + contract_cols(value_back, projected_values)
    )
    normed_one_grad, forward_gain_sum = (
        lax.psum(normed_one_part.astype(jnp.bfloat16), TP).astype(jnp.float32),
        lax.psum(forward_gain_part.astype(jnp.bfloat16), TP).astype(jnp.float32),
    )
    mixer_back, mixer_gain_part = norm_back(stream_in, inverse_one, mixer_scale, normed_one_grad)
    input_field = (stream_grad + mixer_back).reshape(sequence_count, sequence_rows, model_width)
    shards = (
        lax.psum_scatter(
            query_wgrad.astype(jnp.bfloat16), (DP, CX), scatter_dimension=0, tiled=True
        ).astype(jnp.float32),
        lax.psum_scatter(
            key_wgrad.astype(jnp.bfloat16), (DP, CX), scatter_dimension=0, tiled=True
        ).astype(jnp.float32),
        lax.psum_scatter(
            value_wgrad.astype(jnp.bfloat16), (DP, CX), scatter_dimension=0, tiled=True
        ).astype(jnp.float32),
        lax.psum_scatter(
            output_grad.astype(jnp.bfloat16), (DP, CX), scatter_dimension=1, tiled=True
        ).astype(jnp.float32),
        lax.psum_scatter(
            gate_grad.astype(jnp.bfloat16), (DP, CX), scatter_dimension=0, tiled=True
        ).astype(jnp.float32),
        lax.psum_scatter(
            up_grad.astype(jnp.bfloat16), (DP, CX), scatter_dimension=0, tiled=True
        ).astype(jnp.float32),
        lax.psum_scatter(
            down_grad.astype(jnp.bfloat16), (DP, CX), scatter_dimension=1, tiled=True
        ).astype(jnp.float32),
        lax.psum_scatter(
            mixer_gain_part.astype(jnp.bfloat16), (DP, CX), scatter_dimension=0, tiled=True
        ).astype(jnp.float32),
        lax.psum_scatter(
            forward_gain_sum.astype(jnp.bfloat16),
            (DP, CX),
            scatter_dimension=0,
            tiled=True,
        ).astype(jnp.float32),
    )
    masters = (
        query_weight,
        key_weight,
        value_projection,
        output_weight,
        gate_weight,
        up_weight,
        down_weight,
        attention_gain,
        feedforward_gain,
    )
    moments_one = (
        query_weight_first,
        key_projection_first_moment,
        value_projection_first_moment,
        output_weight_first,
        gate_weight_first,
        up_weight_first,
        down_weight_first,
        attention_gain_first,
        feedforward_gain_first,
    )
    moments_two = (
        query_weight_second,
        key_projection_second_moment,
        value_projection_second_moment,
        output_weight_second,
        gate_weight_second,
        up_weight_second,
        down_weight_second,
        attention_gain_second,
        feedforward_gain_second,
    )
    matrix_rate = 1.0 / math.sqrt(MODEL_DIMENSION)
    output_rate = 1.0 / math.sqrt(8 * QUERY_HEADS * HEAD_DIMENSION // full_rows)
    rates = (matrix_rate,) * 3 + (output_rate,) + (matrix_rate,) * 3 + (gain_rate,) * 2
    decays = (decay_rate,) * 7 + (0.0,) * 2
    updates = [
        adamw_update(weight, gradient, moment_one, moment_two, rate_value, decay_value)
        for weight, gradient, moment_one, moment_two, rate_value, decay_value in zip(
            masters, shards, moments_one, moments_two, rates, decays
        )
    ]
    return (
        output_field,
        input_field,
        shards[0],
        shards[1],
        shards[2],
        shards[3],
        shards[4],
        shards[5],
        shards[6],
        shards[7],
        shards[8],
        updates[0][0],
        updates[1][0],
        updates[2][0],
        updates[3][0],
        updates[4][0],
        updates[5][0],
        updates[6][0],
        updates[7][0],
        updates[8][0],
        updates[0][1],
        updates[1][1],
        updates[2][1],
        updates[3][1],
        updates[4][1],
        updates[5][1],
        updates[6][1],
        updates[7][1],
        updates[8][1],
        updates[0][2],
        updates[1][2],
        updates[2][2],
        updates[3][2],
        updates[4][2],
        updates[5][2],
        updates[6][2],
        updates[7][2],
        updates[8][2],
    )


def hidden_kernel(tile, normed, upstream, both_w, down_w, hidden, dboth, dnormed, acc):
    gate_up = nn(normed[...], both_w[...]).astype(bf16).astype(f32)
    gate, up = gate_up[:, :tile], gate_up[:, tile:]
    sigmoid = 1.0 / (1.0 + jnp.exp(-gate))
    silu = gate * sigmoid
    hidden[...] = (silu * up).astype(bf16)
    dhidden = nn(upstream[...], down_w[...])
    dgate = dhidden * up * sigmoid * (1.0 + gate * (1.0 - sigmoid))
    dboth_low = jnp.concatenate([dgate.astype(bf16), (dhidden * silu).astype(bf16)], axis=1)
    dboth[...] = dboth_low
    step = nt(dboth_low, both_w[...])

    @pl.when(pl.program_id(0) == 0)
    def _():
        acc[...] = step

    @pl.when(pl.program_id(0) > 0)
    def _():
        acc[...] += step

    @pl.when(pl.program_id(0) == pl.num_programs(0) - 1)
    def _():
        dnormed[...] = acc[...].astype(bf16)


def feed_forward(normed, upstream, weights, ff):
    rows, model = normed.shape
    tile = FF_TILE
    tiles = ff // tile
    whole = pl.BlockSpec((rows, model), lambda j: (0, 0))
    return pl.pallas_call(
        functools.partial(hidden_kernel, tile),
        grid=(tiles,),
        in_specs=[
            whole,
            whole,
            pl.BlockSpec((model, 2 * tile), lambda j: (0, j)),
            pl.BlockSpec((model, tile), lambda j: (0, 2 * tiles + j)),
        ],
        out_specs=[
            pl.BlockSpec((rows, tile), lambda j: (0, j)),
            pl.BlockSpec((rows, 2 * tile), lambda j: (0, j)),
            whole,
        ],
        out_shape=[
            jax.ShapeDtypeStruct((rows, ff), bf16),
            jax.ShapeDtypeStruct((rows, 2 * ff), bf16),
            jax.ShapeDtypeStruct((rows, model), bf16),
        ],
        scratch_shapes=[pltpu.VMEM((rows, model), f32)],
        compiler_params=pltpu.CompilerParams(vmem_limit_bytes=56 * 1024 * 1024),
        cost_estimate=LARGE,
        name="feed_forward",
    )(normed, upstream, weights, weights)


def mix_kernel(x, own, other, gain, w_own, w_other, stream, normed):
    total = x[...].astype(f32) + nt(own[...], w_own[...]) + nt(other[...], w_other[...])
    stream[...] = total
    inverse = lax.rsqrt(jnp.mean(total * total, axis=-1, keepdims=True) + norm_eps)
    normed[...] = (total * inverse * gain[...]).astype(bf16)


def mix_heads(x, own, other, gain, weights, first_col):
    rows, model = x.shape
    width = own.shape[1]
    tile = 256
    at = first_col // width
    row_block = lambda cols: pl.BlockSpec((tile, cols), lambda r: (r, 0))
    return pl.pallas_call(
        mix_kernel,
        grid=(rows // tile,),
        in_specs=[
            row_block(model),
            row_block(width),
            row_block(width),
            pl.BlockSpec((1, model), lambda r: (0, 0)),
            pl.BlockSpec((model, width), lambda r: (0, at)),
            pl.BlockSpec((model, width), lambda r: (0, at + 1)),
        ],
        out_specs=[row_block(model), row_block(model)],
        out_shape=[
            jax.ShapeDtypeStruct((rows, model), f32),
            jax.ShapeDtypeStruct((rows, model), bf16),
        ],
        compiler_params=pltpu.CompilerParams(vmem_limit_bytes=48 * 1024 * 1024),
        cost_estimate=SMALL,
        name="mix_heads",
    )(x, own, other, gain, weights, weights)


def stream_back_kernel(stream, upstream, own, other, gain, w, dstream, dlow, dheads):
    values = stream[...]
    inverse = lax.rsqrt(jnp.mean(values * values, axis=-1, keepdims=True) + norm_eps)
    unit = values * inverse
    scaled = gain[...] * (own[...].astype(f32) + other[...].astype(f32))
    back = inverse * (scaled - unit * jnp.mean(scaled * unit, axis=-1, keepdims=True))
    total = upstream[...].astype(f32) + back
    dstream[...] = total
    low = total.astype(bf16)
    dlow[...] = low
    dheads[...] = nn(low, w[...]).astype(bf16).T


def stream_back(other, stream, upstream, own, gain, weights, first_col, width):
    rows, model = stream.shape
    tile = 256
    at = first_col // width
    row_block = pl.BlockSpec((tile, model), lambda r: (r, 0))
    return pl.pallas_call(
        stream_back_kernel,
        grid=(rows // tile,),
        in_specs=[row_block] * 4
        + [pl.BlockSpec((1, model), lambda r: (0, 0)), pl.BlockSpec((model, width), lambda r: (0, at))],
        out_specs=[row_block, row_block, pl.BlockSpec((width, tile), lambda r: (0, r))],
        out_shape=[
            jax.ShapeDtypeStruct((rows, model), f32),
            jax.ShapeDtypeStruct((rows, model), bf16),
            jax.ShapeDtypeStruct((width, rows), bf16),
        ],
        compiler_params=pltpu.CompilerParams(vmem_limit_bytes=48 * 1024 * 1024),
        cost_estimate=LARGE,
        name="stream_back",
    )(stream, upstream, own, other, gain, weights)


def gradient_kernel(count, order, *refs):
    left, right = refs[:2 * count], refs[2 * count:3 * count]
    kept, sent = refs[3 * count:]
    total = 0.0
    for s in range(count):
        rows = jnp.concatenate([left[2 * s][...], left[2 * s + 1][...]], axis=1)
        total = total + lax.dot_general(
            rows, right[s][...], (((0,), (0,)), ((), ())), preferred_element_type=f32
        )
    low = total.astype(bf16)

    @pl.when(pl.program_id(0) == 0)
    def _():
        kept[...] = low

    @pl.when(pl.program_id(0) == 1)
    def _():
        sent[...] = low


def gradient(left, right, order, tile):
    rows, model = left[0].shape
    cols = right[0].shape[1]
    quarter = model // 4
    tiles = cols // tile
    count = len(left)
    left_specs = [
        pl.BlockSpec((rows, quarter), functools.partial(lambda p, h, c, order: (0, order[2 * h + p]), p))
        for p in range(2)
    ]
    return pl.pallas_call(
        functools.partial(gradient_kernel, count),
        grid_spec=pltpu.PrefetchScalarGridSpec(
            num_scalar_prefetch=1,
            grid=(2, tiles),
            in_specs=left_specs * count
            + [pl.BlockSpec((rows, tile), lambda h, c, order: (0, c))] * count,
            out_specs=[
                pl.BlockSpec((2 * quarter, tile), lambda h, c, order: (0, jnp.where(h == 0, c, tiles - 1))),
                pl.BlockSpec((2 * quarter, tile), lambda h, c, order: (0, jnp.where(h == 0, 0, c))),
            ],
        ),
        out_shape=[jax.ShapeDtypeStruct((2 * quarter, cols), bf16)] * 2,
        compiler_params=pltpu.CompilerParams(vmem_limit_bytes=56 * 1024 * 1024),
        cost_estimate=LARGE,
        name="gradient",
    )(order, *[each for part in left for each in (part, part)], *right)


def feed_kernel(hidden, w, out):
    out[...] = nt(hidden[...], w[...]).astype(bf16)


def feed_out(hidden, weights, first_col):
    rows, ff = hidden.shape
    model = weights.shape[0]
    tile = 512
    return pl.pallas_call(
        feed_kernel,
        grid=(model // tile,),
        in_specs=[
            pl.BlockSpec((rows, ff), lambda c: (0, 0)),
            pl.BlockSpec((tile, ff), lambda c: (c, first_col // ff)),
        ],
        out_specs=pl.BlockSpec((rows, tile), lambda c: (0, c)),
        out_shape=jax.ShapeDtypeStruct((rows, model), bf16),
        compiler_params=pltpu.CompilerParams(vmem_limit_bytes=48 * 1024 * 1024),
        cost_estimate=LARGE,
        name="feed_out",
    )(hidden, weights)


def input_back_kernel(q_width, kv_width, odd, dq, kept, first, second, last, cos_t, sin_t, w, dkv, dnormed):
    near = jnp.where(odd[0] == 0, first[0].astype(f32), second[0].astype(f32))
    total = kept[0].astype(f32) + near + last[...].astype(f32)
    cos_part, sin_part = cos_t[...], sin_t[...]
    parts = []
    for h in range(kv_width // HD):
        lead = total[h * HD:h * HD + HALF]
        trail = total[h * HD + HALF:(h + 1) * HD]
        parts += [
            (lead * cos_part + trail * sin_part).astype(bf16),
            (trail * cos_part - lead * sin_part).astype(bf16),
        ]
    parts.append(total[kv_width:].astype(bf16))
    rows = jnp.concatenate(parts, axis=0).T
    dkv[...] = rows
    low = nt(dq[...], w[:, :q_width]) + nt(rows, w[:, q_width:q_width + 2 * kv_width])
    dnormed[...] = low.astype(bf16)


def input_back(dq, odd, kept, arrived, last, cos_t, sin_t, weights):
    rows, q_width = dq.shape
    kv_width = kept.shape[1] // 2
    model = weights.shape[0]
    tile = 256
    table = pl.BlockSpec((HALF, tile), lambda r: (0, r))
    piece = lambda at: pl.BlockSpec((1, 2 * kv_width, tile), lambda r: (at, 0, r))
    return pl.pallas_call(
        functools.partial(input_back_kernel, q_width, kv_width),
        grid=(rows // tile,),
        in_specs=[
            pl.BlockSpec(memory_space=pltpu.SMEM),
            pl.BlockSpec((tile, q_width), lambda r: (r, 0)),
            piece(0),
            piece(0),
            piece(1),
            pl.BlockSpec((2 * kv_width, tile), lambda r: (0, r)),
            table,
            table,
            pl.BlockSpec(weights.shape, lambda r: (0, 0)),
        ],
        out_specs=[
            pl.BlockSpec((tile, 2 * kv_width), lambda r: (r, 0)),
            pl.BlockSpec((tile, model), lambda r: (r, 0)),
        ],
        out_shape=[
            jax.ShapeDtypeStruct((rows, 2 * kv_width), bf16),
            jax.ShapeDtypeStruct((rows, model), bf16),
        ],
        compiler_params=pltpu.CompilerParams(vmem_limit_bytes=48 * 1024 * 1024),
        cost_estimate=LARGE,
        name="input_back",
    )(odd, dq, kept, arrived, arrived, last, cos_t, sin_t, weights)


def output_kernel(stream, feed, other, before, out):
    out[0] = stream[...] + feed[...].astype(f32) + other[...].astype(f32)


def finish_output(other, stream, feed, part, parts, before):
    rows, model = stream.shape
    tile = 256
    block = pl.BlockSpec((tile, model), lambda r: (r, 0))
    return pl.pallas_call(
        output_kernel,
        grid=(rows // tile,),
        in_specs=[block, block, block, pl.BlockSpec(memory_space=pl.ANY)],
        out_specs=pl.BlockSpec((1, tile, model), lambda r: (part, r, 0)),
        out_shape=jax.ShapeDtypeStruct((parts, rows, model), f32),
        input_output_aliases={3: 0} if before.ndim == 3 else {},
        compiler_params=pltpu.CompilerParams(vmem_limit_bytes=32 * 1024 * 1024),
        cost_estimate=LARGE,
        name="finish_output",
    )(stream, feed, other, before)


def input_kernel(dstream, x, own, other, gain, before, out):
    values = x[...].astype(f32)
    inverse = lax.rsqrt(jnp.mean(values * values, axis=-1, keepdims=True) + norm_eps)
    unit = values * inverse
    scaled = gain[...] * (own[...].astype(f32) + other[...].astype(f32))
    back = inverse * (scaled - unit * jnp.mean(scaled * unit, axis=-1, keepdims=True))
    out[0] = dstream[...] + back


def finish_input(other, dstream, x, own, gain, part, parts, before):
    rows, model = dstream.shape
    tile = 256
    block = pl.BlockSpec((tile, model), lambda r: (r, 0))
    return pl.pallas_call(
        input_kernel,
        grid=(rows // tile,),
        in_specs=[block] * 4
        + [pl.BlockSpec((1, model), lambda r: (0, 0)), pl.BlockSpec(memory_space=pl.ANY)],
        out_specs=pl.BlockSpec((1, tile, model), lambda r: (part, r, 0)),
        out_shape=jax.ShapeDtypeStruct((parts, rows, model), f32),
        input_output_aliases={5: 0} if before.ndim == 3 else {},
        compiler_params=pltpu.CompilerParams(vmem_limit_bytes=32 * 1024 * 1024),
        cost_estimate=LARGE,
        name="finish_input",
    )(dstream, x, own, other, gain, before)


def interleave(gate, up):
    rows, ff = gate.shape
    pair = jnp.stack([gate.reshape(rows, -1, FF_TILE), up.reshape(rows, -1, FF_TILE)], axis=2)
    return pair.reshape(rows, 2 * ff)


def exchange(values, axis, step):
    size = lax.axis_size(axis)
    return lax.ppermute(values, axis, [(i, i ^ step) for i in range(size)])


def swap(values):
    return exchange(values, TP, 1)


def ring_blocks(block):
    size = lax.axis_size(CX)
    blocks = [block]
    for _ in range(size - 1):
        blocks.append(lax.ppermute(blocks[-1], CX, [(i, (i + 1) % size) for i in range(size)]))
    return blocks


def add_low(a, b):
    return (a.astype(f32) + b.astype(f32)).astype(bf16)


def after(value, *earlier):
    return lax.optimization_barrier((value,) + earlier)[0]


class Line:
    def __init__(self):
        self.last = ()

    def put(self, function, first, *rest):
        first = lax.optimization_barrier((first,) + self.last)[0]
        result = function(first, *rest)
        self.last = (jax.tree.leaves(result)[0],)
        return result


def core_add(kept, arrived):
    half = kept.shape[0] // 2
    return add_low(kept[half:], arrived[half:]), add_low(kept[:half], arrived[:half])


def copy_kernel(source, out):
    out[...] = source[...]


def copy_out(values):
    return pl.pallas_call(
        copy_kernel,
        out_shape=jax.ShapeDtypeStruct(values.shape, values.dtype),
        cost_estimate=LARGE,
        name="copy_out",
    )(values)


def near_pick(held, low):
    grid = held.reshape(2, 2, held.shape[0] // 4, held.shape[1])
    return lax.dynamic_index_in_dim(grid, low, axis=1, keepdims=False)


def far_pick(pair, high):
    return lax.dynamic_index_in_dim(pair, high, axis=0, keepdims=False)


def line_add(held, arrived):
    total = add_low(held, arrived)
    low = lax.axis_index(CX) % 2
    return near_pick(total, 1 - low), near_pick(total, low)


def near_add(held, arrived):
    total = add_low(held, arrived)
    high = lax.axis_index(CX) // 2
    return far_pick(total, 1 - high), far_pick(total, high)


def far_add(held, arrived):
    return held.astype(f32) + arrived.astype(f32)


def far_part(kept, arrived, odd):
    return add_low(kept[1], jnp.where(odd[0] == 0, arrived[1], arrived[0]))


def join(left, right):
    return tuple(jnp.concatenate(each, axis=1) for each in zip(left, right))


def body(
    tokens, out_grad, span_order,
    query_weight, key_weight, value_projection, output_weight, gate_weight, up_weight, down_weight,
    attention_gain, feedforward_gain, *moments,
):
    moments_one, moments_two = moments[:9], moments[9:]
    shards_axes = (DP, CX)
    sequence_count, sequence_rows, model = tokens.shape
    q_width, kv_width = query_weight.shape[1], key_weight.shape[1]
    ff = gate_weight.shape[1]
    context_size = lax.axis_size(CX)
    span_rows = sequence_rows // 2
    gains_low = jnp.stack([attention_gain, feedforward_gain], axis=1).astype(bf16)

    first_shard = jnp.concatenate(
        [
            query_weight.astype(bf16),
            key_weight.astype(bf16),
            value_projection.astype(bf16),
            jnp.pad(gains_low, ((0, 0), (0, 126))),
        ],
        axis=1,
    )
    head_w = lax.all_gather(first_shard, shards_axes, axis=0, tiled=True)
    out_shard = output_weight.astype(bf16).T
    out_w = lax.all_gather(
        after(jnp.concatenate([out_shard, swap(out_shard)], axis=1), head_w), shards_axes, axis=0, tiled=True
    )
    second_shard = jnp.concatenate(
        [interleave(gate_weight.astype(bf16), up_weight.astype(bf16)), down_weight.astype(bf16).T],
        axis=1,
    )
    gains = head_w[:, q_width + 2 * kv_width:q_width + 2 * kv_width + 2].astype(f32).T
    mixer_scale, forward_scale = gains[0:1], gains[1:2]

    context_index = lax.axis_index(CX)
    ring_slots = jnp.stack(
        [2 * ((context_index - s) % context_size) + t for s in range(context_size) for t in range(2)]
    )
    ring_spans = span_order[ring_slots]
    spans = jnp.concatenate([ring_spans[:2], ring_spans]).astype(jnp.int32)
    positions = (
        spans[:2, None] * span_rows + jnp.arange(span_rows, dtype=jnp.int32)[None, :]
    ).reshape(sequence_rows)
    frequency = rope_base ** (-(jnp.arange(HALF, dtype=f32) * 2.0) / HEAD_DIMENSION)
    angles = frequency[:, None] * positions.astype(f32)[None, :]
    cos_t, sin_t = jnp.cos(angles), jnp.sin(angles)
    odd = (context_index % 2).astype(jnp.int32).reshape(1)
    device = lax.axis_index(DP)
    core, line = device % 2, device // 2
    order = jnp.stack(
        [line * 2 + core, (1 - line) * 2 + core, line * 2 + 1 - core, (1 - line) * 2 + 1 - core]
    ).astype(jnp.int32)

    sequences = range(sequence_count)
    normed_one, queries, blocks = [], [], []
    for s in sequences:
        n1, qt, kv = project(tokens[s], mixer_scale, head_w, cos_t, sin_t, q_width, kv_width)
        normed_one.append(n1)
        queries.append(qt)
        blocks.append(ring_blocks(kv))
    rest_w = lax.all_gather(
        after(second_shard, *[each[0] for each in blocks]), shards_axes, axis=0, tiled=True
    )
    attended = [attention_forward(spans, queries[s], blocks[s]) for s in sequences]
    streams, normed_two = [], []
    for s in sequences:
        own = attended[s][0]
        stream, n2 = mix_heads(tokens[s], own, swap(own), forward_scale, out_w, 0)
        streams.append(stream)
        normed_two.append(n2)
    line = Line()
    hiddens, dboths, dnormed, others = [], [], [], []
    for s in sequences:
        hidden, dboth, dn2 = line.put(feed_forward, normed_two[s], out_grad[s], rest_w, ff)
        hiddens.append(hidden)
        dboths.append(dboth)
        dnormed.append(dn2)
        others.append(swap(line.put(copy_out, dn2)))

    def back(s):
        return line.put(
            stream_back, others[s], streams[s], out_grad[s], dnormed[s], forward_scale, out_w, 0, q_width
        )

    def attend_back(s, dheads):
        return line.put(
            attention_backward, dheads, spans, queries[s], attended[s][1], attended[s][2], cos_t, sin_t, blocks[s]
        )

    grads = lambda left, right, tile: line.put(gradient, left, right, order, tile)
    masters = (
        query_weight, key_weight, value_projection, output_weight, gate_weight, up_weight, down_weight,
        attention_gain, feedforward_gain,
    )
    full_rows = span_order.shape[0] * span_rows
    matrix_rate = 1.0 / math.sqrt(MODEL_DIMENSION)
    output_rate = 1.0 / math.sqrt(8 * QUERY_HEADS * HEAD_DIMENSION // full_rows)
    rates = (matrix_rate,) * 3 + (output_rate,) + (matrix_rate,) * 3 + (gain_rate,) * 2
    decays = (decay_rate,) * 7 + (0.0,) * 2

    def update(at, shard):
        return (shard,) + adamw_update(
            masters[at], shard, moments_one[at], moments_two[at], rates[at], decays[at]
        )

    def finish_down(mine, far):
        return (update(6, far_add(mine, far).T),)

    def finish_both(mine, far):
        total = far_add(mine, far)
        pair = total.reshape(total.shape[0], -1, 2, FF_TILE)
        sums = jnp.sum(total * second_shard[:, :2 * ff].astype(f32), axis=1)
        return update(4, pair[:, :, 0].reshape(-1, ff)), update(5, pair[:, :, 1].reshape(-1, ff)), sums

    def finish_mid(mine, far):
        total = far_add(mine, far)
        query = total[:, q_width:]
        sums = jnp.sum(query * first_shard[:, :q_width].astype(f32), axis=1)
        return update(0, query), update(3, total[:, :q_width].T), sums

    def finish_kv(mine, far):
        total = far_add(mine, far)
        sums = jnp.sum(total * first_shard[:, q_width:q_width + 2 * kv_width].astype(f32), axis=1)
        return update(1, total[:, :kv_width]), update(2, total[:, kv_width:]), sums

    down_kept, down_sent = grads([out_grad[s] for s in sequences], hiddens, GRAD_TILE)
    down_core = exchange(down_sent, DP, 1)
    dstream_a, dlow_a, dheads_a = back(0)
    down_passed, down_held = line.put(core_add, down_kept, down_core)
    down_line = exchange(down_passed, DP, 2)
    dq_a, kept_a, sent_a = attend_back(0, dheads_a)
    arrived_a = exchange(line.put(copy_out, sent_a), CX, 1)
    both_kept, both_sent = grads(normed_two, dboths, GRAD_TILE)
    both_core = exchange(both_sent, DP, 1)
    dstream_b, dlow_b, dheads_b = back(1)
    both_passed, both_held = line.put(core_add, both_kept, both_core)
    both_line = exchange(both_passed, DP, 2)
    last_a = exchange(line.put(far_part, kept_a, arrived_a, odd), CX, 2)
    down_away, down_mine = line.put(line_add, down_held, down_line)
    down_near = exchange(down_away, CX, 1)
    dq_b, kept_b, sent_b = attend_back(1, dheads_b)
    arrived_b = exchange(line.put(copy_out, sent_b), CX, 1)
    feed_a = line.put(feed_out, hiddens[0], rest_w, 2 * ff)
    feed_other_a = swap(feed_a)
    down_away, down_mine = line.put(near_add, down_mine, down_near)
    down_far = exchange(down_away, CX, 2)
    dkv_a, dn1_a = line.put(input_back, dq_a, odd, kept_a, arrived_a, last_a, cos_t, sin_t, head_w)
    dn1_other_a = swap(line.put(copy_out, dn1_a))
    output_parts = grads([dlow_a, dlow_b], [each[0] for each in attended], q_width)
    query_parts = grads(normed_one, [dq_a, dq_b], q_width)
    mid_kept, mid_sent = line.put(join, output_parts, query_parts)
    mid_core = exchange(mid_sent, DP, 1)
    last_b = exchange(line.put(far_part, kept_b, arrived_b, odd), CX, 2)
    output_field = line.put(finish_output, feed_other_a, streams[0], feed_a, 0, sequence_count, order)
    mid_passed, mid_held = line.put(core_add, mid_kept, mid_core)
    mid_line = exchange(mid_passed, DP, 2)
    (down_done,) = line.put(finish_down, down_mine, down_far)
    both_away, both_mine = line.put(line_add, both_held, both_line)
    both_near = exchange(both_away, CX, 1)
    dkv_b, dn1_b = line.put(input_back, dq_b, odd, kept_b, arrived_b, last_b, cos_t, sin_t, head_w)
    kv_kept, kv_sent = grads(normed_one, [dkv_a, dkv_b], 2 * kv_width)
    kv_core = exchange(kv_sent, DP, 1)
    dn1_other_b = swap(line.put(copy_out, dn1_b))
    input_field = line.put(
        finish_input, dn1_other_a, dstream_a, tokens[0], dn1_a, mixer_scale, 0, sequence_count, order
    )
    kv_passed, kv_held = line.put(core_add, kv_kept, kv_core)
    kv_line = exchange(kv_passed, DP, 2)
    mid_away, mid_mine = line.put(line_add, mid_held, mid_line)
    mid_near = exchange(mid_away, CX, 1)
    feed_b = line.put(feed_out, hiddens[1], rest_w, 2 * ff)
    feed_other_b = swap(feed_b)
    both_away, both_mine = line.put(near_add, both_mine, both_near)
    both_far = exchange(both_away, CX, 2)
    kv_away, kv_mine = line.put(line_add, kv_held, kv_line)
    kv_near = exchange(kv_away, CX, 1)
    mid_away, mid_mine = line.put(near_add, mid_mine, mid_near)
    mid_far = exchange(mid_away, CX, 2)
    input_field = line.put(
        finish_input, dn1_other_b, dstream_b, tokens[1], dn1_b, mixer_scale, 1, sequence_count, input_field
    )
    kv_away, kv_mine = line.put(near_add, kv_mine, kv_near)
    kv_far = exchange(kv_away, CX, 2)
    gate_done, up_done, both_sums = line.put(finish_both, both_mine, both_far)
    output_field = line.put(
        finish_output, feed_other_b, streams[1], feed_b, 1, sequence_count, output_field
    )
    query_done, output_done, query_sums = line.put(finish_mid, mid_mine, mid_far)
    key_done, value_done, kv_sums = line.put(finish_kv, kv_mine, kv_far)
    row_sums = jnp.stack([query_sums + kv_sums, both_sums])
    gain_shard = (row_sums + swap(row_sums)) / gains_low.astype(f32).T
    done = (
        query_done, key_done, value_done, output_done, gate_done, up_done, down_done,
        update(7, gain_shard[0]), update(8, gain_shard[1]),
    )
    return (output_field, input_field) + tuple(each[part] for part in range(4) for each in done)


def solution(mesh):
    rows, cols, gains = P((DP, CX), TP), P(TP, (DP, CX)), P((DP, CX))
    stream = P(DP, CX, None)
    params = (rows,) * 3 + (cols,) + (rows,) * 2 + (cols,) + (gains,) * 2
    fast = (
        mesh.shape[TP] == 2
        and mesh.shape[DP] == 4
        and mesh.shape[CX] == 4
        and (KEY_VALUE_HEADS // 2 * HEAD_DIMENSION) % 128 == 0
    )
    return jax.shard_map(
        body if fast else plain_body,
        mesh=mesh,
        in_specs=(stream, stream, P()) + params * 3,
        out_specs=(stream, stream) + params * 4,
        check_vma=False,
    )
```

profile of v0, /device:TPU:0, one launch (start us, length us, event | category | flops | bytes accessed | tf_op | source)
XLA Modules:
  0.0 716.5 jit_solution(11229203444361561637)
XLA Ops:
  12.5 3.0 collective-permute-start.4
  15.5 3.8 collective-permute-done.4
  20.1 50.5 %all-gather.4.cloned.1.call-done.w = bf16[1536,1664]{1,0:T(8,128)(2,1)} async-done(((bf16[96,1664]{1,0:T(8,128)(2,1)}), bf16[1536,1664]{1,0:T(8,128)(2,1)}) %all-gather.4.cloned.1.call-update) | async-done | bytes 5111824 | tf_op jit(solution)/shard_map/all_gather | solution.py:1125
  83.5 6.1 project_heads.2
  92.5 6.1 project_heads.3
  104.1 35.2 %collective-permute-done.refs_1_ = bf16[512,768]{1,0:T(8,128)(2,1)S(1)} collective-permute-done((bf16[512,768]{1,0:T(8,128)(2,1)}, bf16[512,768]{1,0:T(8,128)(2,1)S(1)}, u32[]{:S(2)}, u32[]{:S(2)}) %collective-permute-start) | collective-permute-done | bytes 786464 | tf_op jit(solution)/shard_map/ppermute | solution.py:1028
  139.3 19.2 %collective-permute-done.5.refs_1_ = bf16[512,768]{1,0:T(8,128)(2,1)S(1)} collective-permute-done((bf16[512,768]{1,0:T(8,128)(2,1)}, bf16[512,768]{1,0:T(8,128)(2,1)S(1)}, u32[]{:S(2)}, u32[]{:S(2)}) %collective-permute-start.5) | collective-permute-done | bytes 786464 | tf_op jit(solution)/shard_map/ppermute | solution.py:1028
  158.6 25.3 %collective-permute-done.1.refs_2_ = bf16[512,768]{1,0:T(8,128)(2,1)S(1)} collective-permute-done((bf16[512,768]{1,0:T(8,128)(2,1)S(1)}, bf16[512,768]{1,0:T(8,128)(2,1)S(1)}, u32[]{:S(2)}, u32[]{:S(2)}) %collective-permute-start.1) | collective-permute-done | bytes 786464 | tf_op jit(solution)/shard_map/ppermute | solution.py:1028
  183.8 25.3 %collective-permute-done.6.refs_2_ = bf16[512,768]{1,0:T(8,128)(2,1)S(1)} collective-permute-done((bf16[512,768]{1,0:T(8,128)(2,1)S(1)}, bf16[512,768]{1,0:T(8,128)(2,1)S(1)}, u32[]{:S(2)}, u32[]{:S(2)}) %collective-permute-start.6) | collective-permute-done | bytes 786464 | tf_op jit(solution)/shard_map/ppermute | solution.py:1028
  209.2 25.2 %collective-permute-done.2.refs_3_ = bf16[512,768]{1,0:T(8,128)(2,1)S(1)} collective-permute-done((bf16[512,768]{1,0:T(8,128)(2,1)S(1)}, bf16[512,768]{1,0:T(8,128)(2,1)S(1)}, u32[]{:S(2)}, u32[]{:S(2)}) %collective-permute-start.2) | collective-permute-done | bytes 786464 | tf_op jit(solution)/shard_map/ppermute | solution.py:1028
  236.9 14.9 %attention_forward.2 = (bf16[512,768]{1,0:T(8,128)(2,1)}, bf16[768,512]{1,0:T(8,128)(2,1)S(1)}, f32[8,512]{1,0:T(8,128)S(1)}) custom-call(s32[10]{0:T(128)S(1)} %pad_add_fusion.spans, bf16[768,512]{1,0:T(8,128)(2,1)S(1)} %copy-done.11, bf16[512,768]{1,0:T(8,128)(2,1)S(1)} %copy-done.13, bf16[512,768]{1,0:T(8,128)(2,1)S(1)} %collective-permute-done.refs_1_, ...), custom_call_target="tpu_custom_call" | custom-call | flops 1000 | bytes 1000 | tf_op jit(solution)/shard_map/attention_forward/pallas_call | solution.py:118
  254.2 5.3 collective-permute-done.7.refs_3_
  259.5 14.7 %attention_forward.3 = (bf16[512,768]{1,0:T(8,128)(2,1)}, bf16[768,512]{1,0:T(8,128)(2,1)S(1)}, f32[8,512]{1,0:T(8,128)S(1)}) custom-call(s32[10]{0:T(128)S(1)} %pad_add_fusion.spans, bf16[768,512]{1,0:T(8,128)(2,1)S(1)} %copy-done.18, bf16[512,768]{1,0:T(8,128)(2,1)S(1)} %copy-done.20, bf16[512,768]{1,0:T(8,128)(2,1)S(1)} %collective-permute-done.5.refs_1_, ...), custom_call_target="tpu_custom_call" | custom-call | flops 1000 | bytes 1000 | tf_op jit(solution)/shard_map/attention_forward/pallas_call | solution.py:118
  277.8 3.8 slice_bitcast_fusion
  281.6 7.0 mix_heads.2
  289.8 5.4 collective-permute-done.8.other
  295.2 7.0 mix_heads.3
  303.4 15.7 %all-gather.8.cloned.1.call-done.both_w.down_w.w = bf16[1536,6144]{1,0:T(8,128)(2,1)} async-done(((bf16[96,6144]{1,0:T(8,128)(2,1)}), bf16[1536,6144]{1,0:T(8,128)(2,1)}) %all-gather.8.cloned.1.call-update) | async-done | bytes 18874384 | tf_op jit(solution)/shard_map/all_gather | solution.py:1163
  319.0 24.6 %feed_forward.2 = (bf16[512,2048]{1,0:T(8,128)(2,1)}, bf16[512,4096]{1,0:T(8,128)(2,1)}, bf16[512,1536]{1,0:T(8,128)(2,1)}) custom-call(bf16[512,1536]{1,0:T(8,128)(2,1)} %copy-done.38, bf16[512,1536]{1,0:T(8,128)(2,1)} %get-tuple-element.156.upstream.refs_0_.refs_1_, bf16[1536,6144]{1,0:T(8,128)(2,1)} %all-gather.8.cloned.1.call-done.both_w.down_w.w, ...), custom_call_target="tpu_custom_call" | custom-call | flops 999999995904 | bytes 1000 | tf_op jit(solution)/shard_map/feed_forward/pallas_call | solution.py:739
  347.8 24.4 %feed_forward.3 = (bf16[512,2048]{1,0:T(8,128)(2,1)}, bf16[512,4096]{1,0:T(8,128)(2,1)}, bf16[512,1536]{1,0:T(8,128)(2,1)}) custom-call(bf16[512,1536]{1,0:T(8,128)(2,1)} %copy-done.37, bf16[512,1536]{1,0:T(8,128)(2,1)} %get-tuple-element.157.upstream.refs_2_.refs_3_, bf16[1536,6144]{1,0:T(8,128)(2,1)} %all-gather.8.cloned.1.call-done.both_w.down_w.w, ...), custom_call_target="tpu_custom_call" | custom-call | flops 999999995904 | bytes 1000 | tf_op jit(solution)/shard_map/feed_forward/pallas_call | solution.py:739
  375.4 13.3 %gradient.5 = (bf16[768,2048]{1,0:T(8,128)(2,1)}, bf16[768,2048]{1,0:T(8,128)(2,1)}) custom-call(s32[4]{0:T(128)} %pad_add_fusion.1.order.before, bf16[512,1536]{1,0:T(8,128)(2,1)} %get-tuple-element.156.upstream.refs_0_.refs_1_, bf16[512,1536]{1,0:T(8,128)(2,1)} %get-tuple-element.156.upstream.refs_0_.refs_1_, ...), custom_call_target="tpu_custom_call" | custom-call | flops 999999995904 | bytes 1000 | tf_op jit(solution)/shard_map/gradient/pallas_call | solution.py:865
  388.8 6.4 stream_back.2
  395.2 7.0 add_convert_fusion.5
  402.9 19.4 %attention_backward.2 = (bf16[512,768]{1,0:T(8,128)(2,1)}, bf16[2,768,512]{2,1,0:T(8,128)(2,1)}, bf16[2,768,512]{2,1,0:T(8,128)(2,1)}) custom-call(s32[10]{0:T(128)} %copy-done.30, bf16[768,512]{1,0:T(8,128)(2,1)} %copy-done.17, bf16[768,512]{1,0:T(8,128)(2,1)} %copy-done.56, bf16[768,512]{1,0:T(8,128)(2,1)} %copy-done.40, f32[8,512]{1,0:T(8,128)} %copy-done.42, ...), custom_call_target="tpu_custom_call" | custom-call | flops 999999995904 | bytes 1000 | tf_op jit(solution)/shard_map/attention_backward/pallas_call | solution.py:215
  425.6 21.7 %gradient.6 = (bf16[768,4096]{1,0:T(8,128)(2,1)}, bf16[768,4096]{1,0:T(8,128)(2,1)}) custom-call(s32[4]{0:T(128)} %pad_add_fusion.1.order.before, bf16[512,1536]{1,0:T(8,128)(2,1)} %copy-done.38, bf16[512,1536]{1,0:T(8,128)(2,1)} %copy-done.38, bf16[512,1536]{1,0:T(8,128)(2,1)} %copy-done.37, bf16[512,1536]{1,0:T(8,128)(2,1)} %copy-done.37, ...), custom_call_target="tpu_custom_call" | custom-call | flops 999999995904 | bytes 1000 | tf_op jit(solution)/shard_map/gradient/pallas_call | solution.py:865
  447.4 6.0 stream_back.3
  453.4 4.4 collective-permute-done.12
  457.9 7.8 %add_convert_fusion.1 = (bf16[384,4096]{1,0:T(8,128)(2,1)}, bf16[384,4096]{1,0:T(8,128)(2,1)}) fusion(bf16[768,4096]{1,0:T(8,128)(2,1)} %collective-permute-done.12, bf16[768,4096]{1,0:T(8,128)(2,1)} %get-tuple-element.180), kind=kLoop, calls=%fused_computation.2 | loop fusion | flops 12582912 | bytes 18874368 | tf_op jit(solution)/shard_map/convert_element_type | solution.py:1033
  473.8 19.4 %attention_backward.3 = (bf16[512,768]{1,0:T(8,128)(2,1)}, bf16[2,768,512]{2,1,0:T(8,128)(2,1)}, bf16[2,768,512]{2,1,0:T(8,128)(2,1)}) custom-call(s32[10]{0:T(128)} %copy-done.30, bf16[768,512]{1,0:T(8,128)(2,1)} %copy-done.10, bf16[768,512]{1,0:T(8,128)(2,1)} %copy-done.55, bf16[768,512]{1,0:T(8,128)(2,1)} %copy-done.39, f32[8,512]{1,0:T(8,128)} %copy-done.41, ...), custom_call_target="tpu_custom_call" | custom-call | flops 999999995904 | bytes 1000 | tf_op jit(solution)/shard_map/attention_backward/pallas_call | solution.py:215
  498.7 6.9 feed_out.2.feed
  513.1 6.3 input_back.2
  525.4 7.3 %gradient.7 = (bf16[768,768]{1,0:T(8,128)(2,1)}, bf16[768,768]{1,0:T(8,128)(2,1)}) custom-call(s32[4]{0:T(128)} %pad_add_fusion.1.order.before, bf16[512,1536]{1,0:T(8,128)(2,1)} %copy-done.53, bf16[512,1536]{1,0:T(8,128)(2,1)} %copy-done.53, bf16[512,1536]{1,0:T(8,128)(2,1)} %copy-done.54, bf16[512,1536]{1,0:T(8,128)(2,1)} %copy-done.54, ...), custom_call_target="tpu_custom_call" | custom-call | flops 999999995904 | bytes 1000 | tf_op jit(solution)/shard_map/gradient/pallas_call | solution.py:865
  532.7 7.4 %gradient.8 = (bf16[768,768]{1,0:T(8,128)(2,1)}, bf16[768,768]{1,0:T(8,128)(2,1)}) custom-call(s32[4]{0:T(128)} %pad_add_fusion.1.order.before, bf16[512,1536]{1,0:T(8,128)(2,1)} %copy-done.36, bf16[512,1536]{1,0:T(8,128)(2,1)} %copy-done.36, bf16[512,1536]{1,0:T(8,128)(2,1)} %copy-done.35, bf16[512,1536]{1,0:T(8,128)(2,1)} %copy-done.35, ...), custom_call_target="tpu_custom_call" | custom-call | flops 999999995904 | bytes 1000 | tf_op jit(solution)/shard_map/gradient/pallas_call | solution.py:865
  545.4 5.2 collective-permute-done.18.first.second
  554.0 3.2 finish_output.2.before
  557.3 4.5 add_convert_fusion.9
  568.1 3.1 add_convert_fusion
  574.2 17.1 %collective-permute-done.22.last = bf16[768,512]{1,0:T(8,128)(2,1)} collective-permute-done((bf16[768,512]{1,0:T(8,128)(2,1)}, bf16[768,512]{1,0:T(8,128)(2,1)}, u32[]{:S(2)}, u32[]{:S(2)}) %collective-permute-start.22) | collective-permute-done | bytes 786464 | tf_op jit(solution)/shard_map/ppermute | solution.py:1017
  591.3 5.9 input_back.3
  599.3 7.3 %gradient.9 = (bf16[768,768]{1,0:T(8,128)(2,1)}, bf16[768,768]{1,0:T(8,128)(2,1)}) custom-call(s32[4]{0:T(128)} %pad_add_fusion.1.order.before, bf16[512,1536]{1,0:T(8,128)(2,1)} %copy-done.36, bf16[512,1536]{1,0:T(8,128)(2,1)} %copy-done.36, bf16[512,1536]{1,0:T(8,128)(2,1)} %copy-done.35, bf16[512,1536]{1,0:T(8,128)(2,1)} %copy-done.35, ...), custom_call_target="tpu_custom_call" | custom-call | flops 999999995904 | bytes 1000 | tf_op jit(solution)/shard_map/gradient/pallas_call | solution.py:865
  614.1 4.2 finish_input.2.before
  624.9 6.9 feed_out.3.feed
  635.6 3.0 collective-permute-start.32
  646.9 4.0 finish_input.3
  650.9 12.4 %collective-permute-done.31 = bf16[2,96,768]{2,1,0:T(8,128)(2,1)} collective-permute-done((bf16[2,96,768]{2,1,0:T(8,128)(2,1)}, bf16[2,96,768]{2,1,0:T(8,128)(2,1)}, u32[]{:S(2)}, u32[]{:S(2)}) %collective-permute-start.31) | collective-permute-done | bytes 294944 | tf_op jit(solution)/shard_map/ppermute | solution.py:1017
  667.3 16.3 %collective-permute-done.32 = bf16[96,4096]{1,0:T(8,128)(2,1)} collective-permute-done((bf16[96,4096]{1,0:T(8,128)(2,1)}, bf16[96,4096]{1,0:T(8,128)(2,1)}, u32[]{:S(2)}, u32[]{:S(2)}) %collective-permute-start.32) | collective-permute-done | bytes 786464 | tf_op jit(solution)/shard_map/ppermute | solution.py:1017
  687.3 4.5 slice_reduce_fusion
  698.5 3.3 finish_output.3
  (384 shorter events, 144.4 us)
Async XLA Ops:
  7.2 63.6 %copy-start = (s32[8]{0:T(128)S(1)}, s32[8]{0:T(128)}, u32[]{:S(2)}) copy-start(s32[8]{0:T(128)} %param.32) | copy-start | bytes 100
  7.2 63.3 %all-gather.4.cloned.1.call-start = ((), (), s32[]{:S(2)}) async-start(), calls=%async_computation | async-start | bytes 5431296 | tf_op jit(solution)/shard_map/all_gather | solution.py:1125
  9.6 61.8 %copy-start.96 = (bf16[96,384]{1,0:T(8,128)(2,1)}, bf16[96,384]{1,0:T(8,128)(2,1)S(1)}, u32[]{:S(2)}) copy-start(bf16[96,384]{1,0:T(8,128)(2,1)S(1)} %convert_element_type.243) | copy-start | bytes 221188
  10.6 60.9 %copy-start.98 = (bf16[96,384]{1,0:T(8,128)(2,1)}, bf16[96,384]{1,0:T(8,128)(2,1)S(1)}, u32[]{:S(2)}) copy-start(bf16[96,384]{1,0:T(8,128)(2,1)S(1)} %convert_element_type.242) | copy-start | bytes 221188
  11.6 60.0 %copy-start.72 = (f32[96,2048]{1,0:T(8,128)S(1)}, f32[96,2048]{1,0:T(8,128)}, u32[]{:S(2)}) copy-start(f32[96,2048]{1,0:T(8,128)} %param.38) | copy-start | bytes 2359300
  12.4 269.2 %all-gather.6.cloned.1.call-start = ((), (), s32[]{:S(2)}) async-start(), calls=%async_computation.1 | async-start | bytes 5013504 | tf_op jit(solution)/shard_map/all_gather | solution.py:1127
  12.5 6.9 collective-permute-start.4
  70.6 248.5 %all-gather.8.cloned.1.call-start = ((), (), s32[]{:S(2)}) async-start(), calls=%async_computation.2 | async-start | bytes 20054016 | tf_op jit(solution)/shard_map/all_gather | solution.py:1163
  101.6 37.7 %collective-permute-start = (bf16[512,768]{1,0:T(8,128)(2,1)}, bf16[512,768]{1,0:T(8,128)(2,1)S(1)}, u32[]{:S(2)}, u32[]{:S(2)}) collective-permute-start(bf16[512,768]{1,0:T(8,128)(2,1)} %copy-done.12), channel_id=1, source_target_pairs={{0,1},{1,2},{2,3},{3,0},{4,5},{5,6},{6,7},{7,4},{8,9},{9,10},{10,1... | collective-permute-start | bytes 2359304 | tf_op jit(solution)/shard_map/ppermute | solution.py:1028
  103.2 55.4 %collective-permute-start.5 = (bf16[512,768]{1,0:T(8,128)(2,1)}, bf16[512,768]{1,0:T(8,128)(2,1)S(1)}, u32[]{:S(2)}, u32[]{:S(2)}) collective-permute-start(bf16[512,768]{1,0:T(8,128)(2,1)} %copy-done.19), channel_id=1, source_target_pairs={{0,1},{1,2},{2,3},{3,0},{4,5},{5,6},{6,7},{7,4},{8,9},{9,10},{10,1... | collective-permute-start | bytes 2359304 | tf_op jit(solution)/shard_map/ppermute | solution.py:1028
  139.3 112.5 %copy-start.14 = (bf16[512,768]{1,0:T(8,128)(2,1)}, bf16[512,768]{1,0:T(8,128)(2,1)S(1)}, u32[]{:S(2)}) copy-start(bf16[512,768]{1,0:T(8,128)(2,1)S(1)} %collective-permute-done.refs_1_) | copy-start | bytes 2359300
  139.3 44.5 %collective-permute-start.1 = (bf16[512,768]{1,0:T(8,128)(2,1)S(1)}, bf16[512,768]{1,0:T(8,128)(2,1)S(1)}, u32[]{:S(2)}, u32[]{:S(2)}) collective-permute-start(bf16[512,768]{1,0:T(8,128)(2,1)S(1)} %collective-permute-done.refs_1_), channel_id=1, source_target_pairs={{0,1},{1,2},{2,3},{3,0},{4,5},{5,6},{6,7},{7,4},{8,9},{9,10},{10,1... | collective-permute-start | bytes 2359304 | tf_op jit(solution)/shard_map/ppermute | solution.py:1028
  158.5 100.9 %copy-start.21 = (bf16[512,768]{1,0:T(8,128)(2,1)}, bf16[512,768]{1,0:T(8,128)(2,1)S(1)}, u32[]{:S(2)}) copy-start(bf16[512,768]{1,0:T(8,128)(2,1)S(1)} %collective-permute-done.5.refs_1_) | copy-start | bytes 2359300
  158.6 50.6 %collective-permute-start.6 = (bf16[512,768]{1,0:T(8,128)(2,1)S(1)}, bf16[512,768]{1,0:T(8,128)(2,1)S(1)}, u32[]{:S(2)}, u32[]{:S(2)}) collective-permute-start(bf16[512,768]{1,0:T(8,128)(2,1)S(1)} %collective-permute-done.5.refs_1_), channel_id=1, source_target_pairs={{0,1},{1,2},{2,3},{3,0},{4,5},{5,6},{6,7},{7,4},{8,9},{9,10},{10,1... | collective-permute-start | bytes 2359304 | tf_op jit(solution)/shard_map/ppermute | solution.py:1028
  183.8 68.0 %copy-start.15 = (bf16[512,768]{1,0:T(8,128)(2,1)}, bf16[512,768]{1,0:T(8,128)(2,1)S(1)}, u32[]{:S(2)}) copy-start(bf16[512,768]{1,0:T(8,128)(2,1)S(1)} %collective-permute-done.1.refs_2_) | copy-start | bytes 2359300
  183.8 50.6 %collective-permute-start.2 = (bf16[512,768]{1,0:T(8,128)(2,1)S(1)}, bf16[512,768]{1,0:T(8,128)(2,1)S(1)}, u32[]{:S(2)}, u32[]{:S(2)}) collective-permute-start(bf16[512,768]{1,0:T(8,128)(2,1)S(1)} %collective-permute-done.1.refs_2_), channel_id=1, source_target_pairs={{0,1},{1,2},{2,3},{3,0},{4,5},{5,6},{6,7},{7,4},{8,9},{9,10},{10,1... | collective-permute-start | bytes 2359304 | tf_op jit(solution)/shard_map/ppermute | solution.py:1028
  209.1 50.3 %copy-start.22 = (bf16[512,768]{1,0:T(8,128)(2,1)}, bf16[512,768]{1,0:T(8,128)(2,1)S(1)}, u32[]{:S(2)}) copy-start(bf16[512,768]{1,0:T(8,128)(2,1)S(1)} %collective-permute-done.6.refs_2_) | copy-start | bytes 2359300
  209.1 50.3 %collective-permute-start.7 = (bf16[512,768]{1,0:T(8,128)(2,1)S(1)}, bf16[512,768]{1,0:T(8,128)(2,1)S(1)}, u32[]{:S(2)}, u32[]{:S(2)}) collective-permute-start(bf16[512,768]{1,0:T(8,128)(2,1)S(1)} %collective-permute-done.6.refs_2_), channel_id=1, source_target_pairs={{0,1},{1,2},{2,3},{3,0},{4,5},{5,6},{6,7},{7,4},{8,9},{9,10},{10,1... | collective-permute-start | bytes 2359304 | tf_op jit(solution)/shard_map/ppermute | solution.py:1028
  209.2 50.3 %copy-start.30 = (s32[10]{0:T(128)}, s32[10]{0:T(128)S(1)}, u32[]{:S(2)}) copy-start(s32[10]{0:T(128)S(1)} %pad_add_fusion.spans) | copy-start | bytes 124
  252.7 28.9 %collective-permute-start.3 = (bf16[512,768]{1,0:T(8,128)(2,1)}, bf16[512,768]{1,0:T(8,128)(2,1)}, u32[]{:S(2)}, u32[]{:S(2)}) collective-permute-start(bf16[512,768]{1,0:T(8,128)(2,1)} %get-tuple-element.139.own.refs_5_), channel_id=1, source_target_pairs={{0,16},{16,0},{1,17},{17,1},{2,18},{18,2},{3,19},{19,3},{4,20},{20... | collective-permute-start | bytes 2359304 | tf_op jit(solution)/shard_map/ppermute | solution.py:1017
  275.8 19.4 %collective-permute-start.8 = (bf16[512,768]{1,0:T(8,128)(2,1)}, bf16[512,768]{1,0:T(8,128)(2,1)}, u32[]{:S(2)}, u32[]{:S(2)}) collective-permute-start(bf16[512,768]{1,0:T(8,128)(2,1)} %get-tuple-element.145.own.refs_4_), channel_id=1, source_target_pairs={{0,16},{16,0},{1,17},{17,1},{2,18},{18,2},{3,19},{19,3},{4,20},{20... | collective-permute-start | bytes 2359304 | tf_op jit(solution)/shard_map/ppermute | solution.py:1017
  346.3 42.5 %collective-permute-start.9 = (bf16[512,1536]{1,0:T(8,128)(2,1)}, bf16[512,1536]{1,0:T(8,128)(2,1)}, u32[]{:S(2)}, u32[]{:S(2)}) collective-permute-start(bf16[512,1536]{1,0:T(8,128)(2,1)} %copy_out.6), channel_id=1, source_target_pairs={{0,16},{16,0},{1,17},{17,1},{2,18},{18,2},{3,19},{19,3},{4,20},{20... | collective-permute-start | bytes 4718600 | tf_op jit(solution)/shard_map/ppermute | solution.py:1017
  374.9 72.4 %collective-permute-start.10 = (bf16[512,1536]{1,0:T(8,128)(2,1)}, bf16[512,1536]{1,0:T(8,128)(2,1)}, u32[]{:S(2)}, u32[]{:S(2)}) collective-permute-start(bf16[512,1536]{1,0:T(8,128)(2,1)} %copy_out.7), channel_id=1, source_target_pairs={{0,16},{16,0},{1,17},{17,1},{2,18},{18,2},{3,19},{19,3},{4,20},{20... | collective-permute-start | bytes 4718600 | tf_op jit(solution)/shard_map/ppermute | solution.py:1017
  388.7 6.5 collective-permute-start.11
  402.2 67.5 %collective-permute-start.14 = (bf16[384,2048]{1,0:T(8,128)(2,1)}, bf16[384,2048]{1,0:T(8,128)(2,1)}, u32[]{:S(2)}, u32[]{:S(2)}) collective-permute-start(bf16[384,2048]{1,0:T(8,128)(2,1)} %get-tuple-element.351), channel_id=1, source_target_pairs={{0,8},{4,12},{8,0},{12,4},{1,9},{5,13},{9,1},{13,5},{2,10},{6,14},... | collective-permute-start | bytes 4718600 | tf_op jit(solution)/shard_map/ppermute | solution.py:1017
  425.0 40.7 %collective-permute-start.13 = (bf16[2,768,512]{2,1,0:T(8,128)(2,1)}, bf16[2,768,512]{2,1,0:T(8,128)(2,1)}, u32[]{:S(2)}, u32[]{:S(2)}) collective-permute-start(bf16[2,768,512]{2,1,0:T(8,128)(2,1)} %copy_out.8), channel_id=1, source_target_pairs={{0,1},{1,0},{2,3},{3,2},{4,5},{5,4},{6,7},{7,6},{8,9},{9,8},{10,11... | collective-permute-start | bytes 4718600 | tf_op jit(solution)/shard_map/ppermute | solution.py:1017
  447.3 10.6 %collective-permute-start.12 = (bf16[768,4096]{1,0:T(8,128)(2,1)}, bf16[768,4096]{1,0:T(8,128)(2,1)}, u32[]{:S(2)}, u32[]{:S(2)}) collective-permute-start(bf16[768,4096]{1,0:T(8,128)(2,1)} %get-tuple-element.181), channel_id=1, source_target_pairs={{0,4},{4,0},{8,12},{12,8},{1,5},{5,1},{9,13},{13,9},{2,6},{6,2},{1... | collective-permute-start | bytes 18874376 | tf_op jit(solution)/shard_map/ppermute | solution.py:1017
  468.4 44.6 %collective-permute-start.16 = (bf16[768,512]{1,0:T(8,128)(2,1)}, bf16[768,512]{1,0:T(8,128)(2,1)}, u32[]{:S(2)}, u32[]{:S(2)}) collective-permute-start(bf16[768,512]{1,0:T(8,128)(2,1)} %fusion.3), channel_id=1, source_target_pairs={{0,2},{1,3},{2,0},{3,1},{4,6},{5,7},{6,4},{7,5},{8,10},{9,11},{10,... | collective-permute-start | bytes 2359304 | tf_op jit(solution)/shard_map/ppermute | solution.py:1017
  473.0 36.6 %collective-permute-start.15 = (bf16[2,96,2048]{2,1,0:T(8,128)(2,1)}, bf16[2,96,2048]{2,1,0:T(8,128)(2,1)}, u32[]{:S(2)}, u32[]{:S(2)}) collective-permute-start(bf16[2,96,2048]{2,1,0:T(8,128)(2,1)} %get-tuple-element.367), channel_id=1, source_target_pairs={{0,1},{1,0},{2,3},{3,2},{4,5},{5,4},{6,7},{7,6},{8,9},{9,8},{10,11... | collective-permute-start | bytes 2359304 | tf_op jit(solution)/shard_map/ppermute | solution.py:1017
  495.8 54.8 %collective-permute-start.18 = (bf16[2,768,512]{2,1,0:T(8,128)(2,1)}, bf16[2,768,512]{2,1,0:T(8,128)(2,1)}, u32[]{:S(2)}, u32[]{:S(2)}) collective-permute-start(bf16[2,768,512]{2,1,0:T(8,128)(2,1)} %copy_out.9), channel_id=1, source_target_pairs={{0,1},{1,0},{2,3},{3,2},{4,5},{5,4},{6,7},{7,6},{8,9},{9,8},{10,11... | collective-permute-start | bytes 4718600 | tf_op jit(solution)/shard_map/ppermute | solution.py:1017
  497.1 71.0 %collective-permute-start.21 = (bf16[384,4096]{1,0:T(8,128)(2,1)}, bf16[384,4096]{1,0:T(8,128)(2,1)}, u32[]{:S(2)}, u32[]{:S(2)}) collective-permute-start(bf16[384,4096]{1,0:T(8,128)(2,1)} %get-tuple-element.349), channel_id=1, source_target_pairs={{0,8},{4,12},{8,0},{12,4},{1,9},{5,13},{9,1},{13,5},{2,10},{6,14},... | collective-permute-start | bytes 9437192 | tf_op jit(solution)/shard_map/ppermute | solution.py:1017
  505.6 47.6 %collective-permute-start.17 = (bf16[512,1536]{1,0:T(8,128)(2,1)}, bf16[512,1536]{1,0:T(8,128)(2,1)}, u32[]{:S(2)}, u32[]{:S(2)}) collective-permute-start(bf16[512,1536]{1,0:T(8,128)(2,1)} %feed_out.2.feed), channel_id=1, source_target_pairs={{0,16},{16,0},{1,17},{17,1},{2,18},{18,2},{3,19},{19,3},{4,20},{20... | collective-permute-start | bytes 4718600 | tf_op jit(solution)/shard_map/ppermute | solution.py:1017
  512.0 51.9 %collective-permute-start.20 = (bf16[96,2048]{1,0:T(8,128)(2,1)}, bf16[96,2048]{1,0:T(8,128)(2,1)}, u32[]{:S(2)}, u32[]{:S(2)}) collective-permute-start(bf16[96,2048]{1,0:T(8,128)(2,1)} %get-tuple-element.371), channel_id=1, source_target_pairs={{0,2},{1,3},{2,0},{3,1},{4,6},{5,7},{6,4},{7,5},{8,10},{9,11},{10,... | collective-permute-start | bytes 1179656 | tf_op jit(solution)/shard_map/ppermute | solution.py:1017
  524.2 86.6 %collective-permute-start.23 = (bf16[512,1536]{1,0:T(8,128)(2,1)}, bf16[512,1536]{1,0:T(8,128)(2,1)}, u32[]{:S(2)}, u32[]{:S(2)}) collective-permute-start(bf16[512,1536]{1,0:T(8,128)(2,1)} %copy_out.10), channel_id=1, source_target_pairs={{0,16},{16,0},{1,17},{17,1},{2,18},{18,2},{3,19},{19,3},{4,20},{20... | collective-permute-start | bytes 4718600 | tf_op jit(solution)/shard_map/ppermute | solution.py:1017
  550.6 6.7 collective-permute-start.19
  553.2 38.1 %collective-permute-start.22 = (bf16[768,512]{1,0:T(8,128)(2,1)}, bf16[768,512]{1,0:T(8,128)(2,1)}, u32[]{:S(2)}, u32[]{:S(2)}) collective-permute-start(bf16[768,512]{1,0:T(8,128)(2,1)} %fusion.4), channel_id=1, source_target_pairs={{0,2},{1,3},{2,0},{3,1},{4,6},{5,7},{6,4},{7,5},{8,10},{9,11},{10,... | collective-permute-start | bytes 2359304 | tf_op jit(solution)/shard_map/ppermute | solution.py:1017
  561.8 59.5 %collective-permute-start.25 = (bf16[384,1536]{1,0:T(8,128)(2,1)}, bf16[384,1536]{1,0:T(8,128)(2,1)}, u32[]{:S(2)}, u32[]{:S(2)}) collective-permute-start(bf16[384,1536]{1,0:T(8,128)(2,1)} %get-tuple-element.353), channel_id=1, source_target_pairs={{0,8},{4,12},{8,0},{12,4},{1,9},{5,13},{9,1},{13,5},{2,10},{6,14},... | collective-permute-start | bytes 3538952 | tf_op jit(solution)/shard_map/ppermute | solution.py:1017
  573.0 59.3 %collective-permute-start.27 = (bf16[2,96,4096]{2,1,0:T(8,128)(2,1)}, bf16[2,96,4096]{2,1,0:T(8,128)(2,1)}, u32[]{:S(2)}, u32[]{:S(2)}) collective-permute-start(bf16[2,96,4096]{2,1,0:T(8,128)(2,1)} %get-tuple-element.355), channel_id=1, source_target_pairs={{0,1},{1,0},{2,3},{3,2},{4,5},{5,4},{6,7},{7,6},{8,9},{9,8},{10,11... | collective-permute-start | bytes 4718600 | tf_op jit(solution)/shard_map/ppermute | solution.py:1017
  606.6 11.7 %collective-permute-start.24 = (bf16[768,768]{1,0:T(8,128)(2,1)}, bf16[768,768]{1,0:T(8,128)(2,1)}, u32[]{:S(2)}, u32[]{:S(2)}) collective-permute-start(bf16[768,768]{1,0:T(8,128)(2,1)} %get-tuple-element.224), channel_id=1, source_target_pairs={{0,4},{4,0},{8,12},{12,8},{1,5},{5,1},{9,13},{13,9},{2,6},{6,2},{1... | collective-permute-start | bytes 3538952 | tf_op jit(solution)/shard_map/ppermute | solution.py:1017
  609.3 37.5 %collective-permute-start.29 = (bf16[512,1536]{1,0:T(8,128)(2,1)}, bf16[512,1536]{1,0:T(8,128)(2,1)}, u32[]{:S(2)}, u32[]{:S(2)}) collective-permute-start(bf16[512,1536]{1,0:T(8,128)(2,1)} %copy_out.11), channel_id=1, source_target_pairs={{0,16},{16,0},{1,17},{17,1},{2,18},{18,2},{3,19},{19,3},{4,20},{20... | collective-permute-start | bytes 4718600 | tf_op jit(solution)/shard_map/ppermute | solution.py:1017
  620.9 17.7 %collective-permute-start.28 = (bf16[384,768]{1,0:T(8,128)(2,1)}, bf16[384,768]{1,0:T(8,128)(2,1)}, u32[]{:S(2)}, u32[]{:S(2)}) collective-permute-start(bf16[384,768]{1,0:T(8,128)(2,1)} %get-tuple-element.361), channel_id=1, source_target_pairs={{0,8},{4,12},{8,0},{12,4},{1,9},{5,13},{9,1},{13,5},{2,10},{6,14},... | collective-permute-start | bytes 1769480 | tf_op jit(solution)/shard_map/ppermute | solution.py:1017
  624.0 17.8 %collective-permute-start.30 = (bf16[2,96,1536]{2,1,0:T(8,128)(2,1)}, bf16[2,96,1536]{2,1,0:T(8,128)(2,1)}, u32[]{:S(2)}, u32[]{:S(2)}) collective-permute-start(bf16[2,96,1536]{2,1,0:T(8,128)(2,1)} %get-tuple-element.369), channel_id=1, source_target_pairs={{0,1},{1,0},{2,3},{3,2},{4,5},{5,4},{6,7},{7,6},{8,9},{9,8},{10,11... | collective-permute-start | bytes 1769480 | tf_op jit(solution)/shard_map/ppermute | solution.py:1017
  631.8 65.8 %collective-permute-start.26 = (bf16[512,1536]{1,0:T(8,128)(2,1)}, bf16[512,1536]{1,0:T(8,128)(2,1)}, u32[]{:S(2)}, u32[]{:S(2)}) collective-permute-start(bf16[512,1536]{1,0:T(8,128)(2,1)} %feed_out.3.feed), channel_id=1, source_target_pairs={{0,16},{16,0},{1,17},{17,1},{2,18},{18,2},{3,19},{19,3},{4,20},{20... | collective-permute-start | bytes 4718600 | tf_op jit(solution)/shard_map/ppermute | solution.py:1017
  635.6 48.0 %collective-permute-start.32 = (bf16[96,4096]{1,0:T(8,128)(2,1)}, bf16[96,4096]{1,0:T(8,128)(2,1)}, u32[]{:S(2)}, u32[]{:S(2)}) collective-permute-start(bf16[96,4096]{1,0:T(8,128)(2,1)} %get-tuple-element.365), channel_id=1, source_target_pairs={{0,2},{1,3},{2,0},{3,1},{4,6},{5,7},{6,4},{7,5},{8,10},{9,11},{10,... | collective-permute-start | bytes 2359304 | tf_op jit(solution)/shard_map/ppermute | solution.py:1017
  640.9 22.4 %collective-permute-start.31 = (bf16[2,96,768]{2,1,0:T(8,128)(2,1)}, bf16[2,96,768]{2,1,0:T(8,128)(2,1)}, u32[]{:S(2)}, u32[]{:S(2)}) collective-permute-start(bf16[2,96,768]{2,1,0:T(8,128)(2,1)} %get-tuple-element.375), channel_id=1, source_target_pairs={{0,1},{1,0},{2,3},{3,2},{4,5},{5,4},{6,7},{7,6},{8,9},{9,8},{10,11... | collective-permute-start | bytes 884744 | tf_op jit(solution)/shard_map/ppermute | solution.py:1017
  643.8 58.0 %collective-permute-start.33 = (bf16[96,1536]{1,0:T(8,128)(2,1)}, bf16[96,1536]{1,0:T(8,128)(2,1)}, u32[]{:S(2)}, u32[]{:S(2)}) collective-permute-start(bf16[96,1536]{1,0:T(8,128)(2,1)} %get-tuple-element.373), channel_id=1, source_target_pairs={{0,2},{1,3},{2,0},{3,1},{4,6},{5,7},{6,4},{7,5},{8,10},{9,11},{10,... | collective-permute-start | bytes 884744 | tf_op jit(solution)/shard_map/ppermute | solution.py:1017
  665.1 39.2 %collective-permute-start.34 = (bf16[96,768]{1,0:T(8,128)(2,1)}, bf16[96,768]{1,0:T(8,128)(2,1)}, u32[]{:S(2)}, u32[]{:S(2)}) collective-permute-start(bf16[96,768]{1,0:T(8,128)(2,1)} %get-tuple-element.383), channel_id=1, source_target_pairs={{0,2},{1,3},{2,0},{3,1},{4,6},{5,7},{6,4},{7,5},{8,10},{9,11},{10,... | collective-permute-start | bytes 442376 | tf_op jit(solution)/shard_map/ppermute | solution.py:1017
  705.5 3.6 collective-permute-start.35
  (113 other events, 682.4 us)
Sparse Core Ops, SparseCore 0:
  12.5 57.9 all-gather.3
  73.4 62.7 all-gather.5
  138.4 180.6 all-gather.7
where the time goes:
time: 726 us; the launch traced here: 716 us
  waiting for transfers between devices  273 us (38%)
  Pallas kernels  270 us (37%)
  other arithmetic  68.5 us (9%)
  local copies, waits for them, and re-layouts  56.1 us (8%)
  starting transfers between devices  34 us (5%)
  between operations  15.3 us (2%)
    ppermute x6, waiting for transfers between devices, ring_blocks(): lax.ppermute(blocks[-1], CX, [(i, (i + 1) % size) for i in range(size)])  135 us
    ppermute x30, waiting for transfers between devices, exchange(): return lax.ppermute(values, axis, [(i, i ^ step) for i in range(size)])  71.1 us
    pallas_call x5, Pallas kernels, gradient(): pl.pallas_call(functools.partial(gradient_kernel, count), grid_spec=pltpu...  57 us
    all_gather x1, waiting for transfers between devices, body(): head_w = lax.all_gather(first_shard, shards_axes, axis=0, tiled=True)  50.5 us
    pallas_call x2, Pallas kernels, feed_forward(): pl.pallas_call(functools.partial(hidden_kernel, tile), grid=(tiles,), in_...  49 us
    convert_element_type x14, other arithmetic, add_low(): return (a.astype(f32) + b.astype(f32)).astype(bf16)  40.8 us
    pallas_call x2, Pallas kernels, attention_backward(): pl.pallas_call(functools.partial(backward_kernel, kv_heads, group, span_r...  38.7 us
    ppermute x30, starting transfers between devices, exchange(): return lax.ppermute(values, axis, [(i, i ^ step) for i in range(size)])  31.4 us
  transfers between devices with their start and end apart: 39, of which 19 were waited for; matrix products, arithmetic and copies ran while one was open for 13% of the time, Pallas kernels for 34%

commit v1 on v0

--- a/solution.py
+++ b/solution.py
@@ -1268,12 +1268,12 @@
     )
     kv_passed, kv_held = line.put(core_add, kv_kept, kv_core)
     kv_line = exchange(kv_passed, DP, 2)
+    both_away, both_mine = line.put(near_add, both_mine, both_near)
+    both_far = exchange(both_away, CX, 2)
     mid_away, mid_mine = line.put(line_add, mid_held, mid_line)
     mid_near = exchange(mid_away, CX, 1)
     feed_b = line.put(feed_out, hiddens[1], rest_w, 2 * ff)
     feed_other_b = swap(feed_b)
-    both_away, both_mine = line.put(near_add, both_mine, both_near)
-    both_far = exchange(both_away, CX, 2)
     kv_away, kv_mine = line.put(line_add, kv_held, kv_line)
     kv_near = exchange(kv_away, CX, 1)
     mid_away, mid_mine = line.put(near_add, mid_mine, mid_near)
@@ -1284,10 +1284,10 @@
     kv_away, kv_mine = line.put(near_add, kv_mine, kv_near)
     kv_far = exchange(kv_away, CX, 2)
     gate_done, up_done, both_sums = line.put(finish_both, both_mine, both_far)
+    query_done, output_done, query_sums = line.put(finish_mid, mid_mine, mid_far)
     output_field = line.put(
         finish_output, feed_other_b, streams[1], feed_b, 1, sequence_count, output_field
     )
-    query_done, output_done, query_sums = line.put(finish_mid, mid_mine, mid_far)
     key_done, value_done, kv_sums = line.put(finish_kv, kv_mine, kv_far)
     row_sums = jnp.stack([query_sums + kv_sums, both_sums])
     gain_shard = (row_sums + swap(row_sums)) / gains_low.astype(f32).T

time: 726 us -> 721 us (level)
    unnamed x250 -> x252, local copies, waits for them, and re-layouts: 30.6 us -> 30.3 us
where the time goes in v1:
time: 721 us; the launch traced here: 707 us
  Pallas kernels  270 us (37%)
  waiting for transfers between devices  267 us (37%)
  other arithmetic  69 us (10%)
  local copies, waits for them, and re-layouts  55.8 us (8%)
  starting transfers between devices  30.7 us (4%)
  between operations  15.3 us (2%)
    ppermute x6, waiting for transfers between devices, ring_blocks(): lax.ppermute(blocks[-1], CX, [(i, (i + 1) % size) for i in range(size)])  135 us
    ppermute x30, waiting for transfers between devices, exchange(): return lax.ppermute(values, axis, [(i, i ^ step) for i in range(size)])  65 us
    pallas_call x5, Pallas kernels, gradient(): pl.pallas_call(functools.partial(gradient_kernel, count), grid_spec=pltpu...  57 us
    all_gather x1, waiting for transfers between devices, body(): head_w = lax.all_gather(first_shard, shards_axes, axis=0, tiled=True)  50.5 us
    pallas_call x2, Pallas kernels, feed_forward(): pl.pallas_call(functools.partial(hidden_kernel, tile), grid=(tiles,), in_...  48.9 us
    convert_element_type x14, other arithmetic, add_low(): return (a.astype(f32) + b.astype(f32)).astype(bf16)  40.8 us
    pallas_call x2, Pallas kernels, attention_backward(): pl.pallas_call(functools.partial(backward_kernel, kv_heads, group, span_r...  38.8 us
    unnamed x252, local copies, waits for them, and re-layouts  30.3 us
  transfers between devices with their start and end apart: 39, of which 19 were waited for; matrix products, arithmetic and copies ran while one was open for 13% of the time, Pallas kernels for 34%

profile of v1, /device:TPU:0, one launch (start us, length us, event | category | flops | bytes accessed | tf_op | source)
XLA Modules:
  0.0 707.5 jit_solution(12423464920183714201)
XLA Ops:
  12.5 3.0 collective-permute-start.4
  15.5 3.8 collective-permute-done.4
  20.1 50.5 %all-gather.4.cloned.1.call-done.w = bf16[1536,1664]{1,0:T(8,128)(2,1)} async-done(((bf16[96,1664]{1,0:T(8,128)(2,1)}), bf16[1536,1664]{1,0:T(8,128)(2,1)}) %all-gather.4.cloned.1.call-update) | async-done | bytes 5111824 | tf_op jit(solution)/shard_map/all_gather | solution.py:1125
  83.5 6.1 project_heads.2
  92.5 6.1 project_heads.3
  104.1 35.2 %collective-permute-done.refs_1_ = bf16[512,768]{1,0:T(8,128)(2,1)S(1)} collective-permute-done((bf16[512,768]{1,0:T(8,128)(2,1)}, bf16[512,768]{1,0:T(8,128)(2,1)S(1)}, u32[]{:S(2)}, u32[]{:S(2)}) %collective-permute-start) | collective-permute-done | bytes 786464 | tf_op jit(solution)/shard_map/ppermute | solution.py:1028
  139.4 19.2 %collective-permute-done.5.refs_1_ = bf16[512,768]{1,0:T(8,128)(2,1)S(1)} collective-permute-done((bf16[512,768]{1,0:T(8,128)(2,1)}, bf16[512,768]{1,0:T(8,128)(2,1)S(1)}, u32[]{:S(2)}, u32[]{:S(2)}) %collective-permute-start.5) | collective-permute-done | bytes 786464 | tf_op jit(solution)/shard_map/ppermute | solution.py:1028
  158.6 25.3 %collective-permute-done.1.refs_2_ = bf16[512,768]{1,0:T(8,128)(2,1)S(1)} collective-permute-done((bf16[512,768]{1,0:T(8,128)(2,1)S(1)}, bf16[512,768]{1,0:T(8,128)(2,1)S(1)}, u32[]{:S(2)}, u32[]{:S(2)}) %collective-permute-start.1) | collective-permute-done | bytes 786464 | tf_op jit(solution)/shard_map/ppermute | solution.py:1028
  183.8 25.3 %collective-permute-done.6.refs_2_ = bf16[512,768]{1,0:T(8,128)(2,1)S(1)} collective-permute-done((bf16[512,768]{1,0:T(8,128)(2,1)S(1)}, bf16[512,768]{1,0:T(8,128)(2,1)S(1)}, u32[]{:S(2)}, u32[]{:S(2)}) %collective-permute-start.6) | collective-permute-done | bytes 786464 | tf_op jit(solution)/shard_map/ppermute | solution.py:1028
  209.2 25.2 %collective-permute-done.2.refs_3_ = bf16[512,768]{1,0:T(8,128)(2,1)S(1)} collective-permute-done((bf16[512,768]{1,0:T(8,128)(2,1)S(1)}, bf16[512,768]{1,0:T(8,128)(2,1)S(1)}, u32[]{:S(2)}, u32[]{:S(2)}) %collective-permute-start.2) | collective-permute-done | bytes 786464 | tf_op jit(solution)/shard_map/ppermute | solution.py:1028
  237.0 14.9 %attention_forward.2 = (bf16[512,768]{1,0:T(8,128)(2,1)}, bf16[768,512]{1,0:T(8,128)(2,1)S(1)}, f32[8,512]{1,0:T(8,128)S(1)}) custom-call(s32[10]{0:T(128)S(1)} %pad_add_fusion.spans, bf16[768,512]{1,0:T(8,128)(2,1)S(1)} %copy-done.11, bf16[512,768]{1,0:T(8,128)(2,1)S(1)} %copy-done.13, bf16[512,768]{1,0:T(8,128)(2,1)S(1)} %collective-permute-done.refs_1_, ...), custom_call_target="tpu_custom_call" | custom-call | flops 1000 | bytes 1000 | tf_op jit(solution)/shard_map/attention_forward/pallas_call | solution.py:118
  254.2 5.3 collective-permute-done.7.refs_3_
  259.5 14.7 %attention_forward.3 = (bf16[512,768]{1,0:T(8,128)(2,1)}, bf16[768,512]{1,0:T(8,128)(2,1)S(1)}, f32[8,512]{1,0:T(8,128)S(1)}) custom-call(s32[10]{0:T(128)S(1)} %pad_add_fusion.spans, bf16[768,512]{1,0:T(8,128)(2,1)S(1)} %copy-done.18, bf16[512,768]{1,0:T(8,128)(2,1)S(1)} %copy-done.20, bf16[512,768]{1,0:T(8,128)(2,1)S(1)} %collective-permute-done.5.refs_1_, ...), custom_call_target="tpu_custom_call" | custom-call | flops 1000 | bytes 1000 | tf_op jit(solution)/shard_map/attention_forward/pallas_call | solution.py:118
  277.8 3.8 slice_bitcast_fusion
  281.6 7.0 mix_heads.2
  289.8 5.4 collective-permute-done.8.other
  295.2 7.0 mix_heads.3
  303.3 15.7 %all-gather.8.cloned.1.call-done.both_w.down_w.w = bf16[1536,6144]{1,0:T(8,128)(2,1)} async-done(((bf16[96,6144]{1,0:T(8,128)(2,1)}), bf16[1536,6144]{1,0:T(8,128)(2,1)}) %all-gather.8.cloned.1.call-update) | async-done | bytes 18874384 | tf_op jit(solution)/shard_map/all_gather | solution.py:1163
  319.0 24.6 %feed_forward.2 = (bf16[512,2048]{1,0:T(8,128)(2,1)}, bf16[512,4096]{1,0:T(8,128)(2,1)}, bf16[512,1536]{1,0:T(8,128)(2,1)}) custom-call(bf16[512,1536]{1,0:T(8,128)(2,1)} %copy-done.38, bf16[512,1536]{1,0:T(8,128)(2,1)} %get-tuple-element.156.upstream.refs_0_.refs_1_, bf16[1536,6144]{1,0:T(8,128)(2,1)} %all-gather.8.cloned.1.call-done.both_w.down_w.w, ...), custom_call_target="tpu_custom_call" | custom-call | flops 999999995904 | bytes 1000 | tf_op jit(solution)/shard_map/feed_forward/pallas_call | solution.py:739
  347.8 24.4 %feed_forward.3 = (bf16[512,2048]{1,0:T(8,128)(2,1)}, bf16[512,4096]{1,0:T(8,128)(2,1)}, bf16[512,1536]{1,0:T(8,128)(2,1)}) custom-call(bf16[512,1536]{1,0:T(8,128)(2,1)} %copy-done.37, bf16[512,1536]{1,0:T(8,128)(2,1)} %get-tuple-element.157.upstream.refs_2_.refs_3_, bf16[1536,6144]{1,0:T(8,128)(2,1)} %all-gather.8.cloned.1.call-done.both_w.down_w.w, ...), custom_call_target="tpu_custom_call" | custom-call | flops 999999995904 | bytes 1000 | tf_op jit(solution)/shard_map/feed_forward/pallas_call | solution.py:739
  375.4 13.3 %gradient.5 = (bf16[768,2048]{1,0:T(8,128)(2,1)}, bf16[768,2048]{1,0:T(8,128)(2,1)}) custom-call(s32[4]{0:T(128)} %pad_add_fusion.1.order.before, bf16[512,1536]{1,0:T(8,128)(2,1)} %get-tuple-element.156.upstream.refs_0_.refs_1_, bf16[512,1536]{1,0:T(8,128)(2,1)} %get-tuple-element.156.upstream.refs_0_.refs_1_, ...), custom_call_target="tpu_custom_call" | custom-call | flops 999999995904 | bytes 1000 | tf_op jit(solution)/shard_map/gradient/pallas_call | solution.py:865
  388.7 6.4 stream_back.2
  395.2 6.9 add_convert_fusion.5
  402.9 19.4 %attention_backward.2 = (bf16[512,768]{1,0:T(8,128)(2,1)}, bf16[2,768,512]{2,1,0:T(8,128)(2,1)}, bf16[2,768,512]{2,1,0:T(8,128)(2,1)}) custom-call(s32[10]{0:T(128)} %copy-done.30, bf16[768,512]{1,0:T(8,128)(2,1)} %copy-done.17, bf16[768,512]{1,0:T(8,128)(2,1)} %copy-done.56, bf16[768,512]{1,0:T(8,128)(2,1)} %copy-done.40, f32[8,512]{1,0:T(8,128)} %copy-done.42, ...), custom_call_target="tpu_custom_call" | custom-call | flops 999999995904 | bytes 1000 | tf_op jit(solution)/shard_map/attention_backward/pallas_call | solution.py:215
  425.5 21.7 %gradient.6 = (bf16[768,4096]{1,0:T(8,128)(2,1)}, bf16[768,4096]{1,0:T(8,128)(2,1)}) custom-call(s32[4]{0:T(128)} %pad_add_fusion.1.order.before, bf16[512,1536]{1,0:T(8,128)(2,1)} %copy-done.38, bf16[512,1536]{1,0:T(8,128)(2,1)} %copy-done.38, bf16[512,1536]{1,0:T(8,128)(2,1)} %copy-done.37, bf16[512,1536]{1,0:T(8,128)(2,1)} %copy-done.37, ...), custom_call_target="tpu_custom_call" | custom-call | flops 999999995904 | bytes 1000 | tf_op jit(solution)/shard_map/gradient/pallas_call | solution.py:865
  447.3 6.0 stream_back.3
  453.4 4.4 collective-permute-done.12
  457.8 7.8 %add_convert_fusion.1 = (bf16[384,4096]{1,0:T(8,128)(2,1)}, bf16[384,4096]{1,0:T(8,128)(2,1)}) fusion(bf16[768,4096]{1,0:T(8,128)(2,1)} %collective-permute-done.12, bf16[768,4096]{1,0:T(8,128)(2,1)} %get-tuple-element.180), kind=kLoop, calls=%fused_computation.2 | loop fusion | flops 12582912 | bytes 18874368 | tf_op jit(solution)/shard_map/convert_element_type | solution.py:1033
  473.7 19.4 %attention_backward.3 = (bf16[512,768]{1,0:T(8,128)(2,1)}, bf16[2,768,512]{2,1,0:T(8,128)(2,1)}, bf16[2,768,512]{2,1,0:T(8,128)(2,1)}) custom-call(s32[10]{0:T(128)} %copy-done.30, bf16[768,512]{1,0:T(8,128)(2,1)} %copy-done.10, bf16[768,512]{1,0:T(8,128)(2,1)} %copy-done.55, bf16[768,512]{1,0:T(8,128)(2,1)} %copy-done.39, f32[8,512]{1,0:T(8,128)} %copy-done.41, ...), custom_call_target="tpu_custom_call" | custom-call | flops 999999995904 | bytes 1000 | tf_op jit(solution)/shard_map/attention_backward/pallas_call | solution.py:215
  498.7 6.9 feed_out.2.feed
  513.1 6.3 input_back.2
  525.3 7.3 %gradient.7 = (bf16[768,768]{1,0:T(8,128)(2,1)}, bf16[768,768]{1,0:T(8,128)(2,1)}) custom-call(s32[4]{0:T(128)} %pad_add_fusion.1.order.before, bf16[512,1536]{1,0:T(8,128)(2,1)} %copy-done.53, bf16[512,1536]{1,0:T(8,128)(2,1)} %copy-done.53, bf16[512,1536]{1,0:T(8,128)(2,1)} %copy-done.54, bf16[512,1536]{1,0:T(8,128)(2,1)} %copy-done.54, ...), custom_call_target="tpu_custom_call" | custom-call | flops 999999995904 | bytes 1000 | tf_op jit(solution)/shard_map/gradient/pallas_call | solution.py:865
  532.6 7.4 %gradient.8 = (bf16[768,768]{1,0:T(8,128)(2,1)}, bf16[768,768]{1,0:T(8,128)(2,1)}) custom-call(s32[4]{0:T(128)} %pad_add_fusion.1.order.before, bf16[512,1536]{1,0:T(8,128)(2,1)} %copy-done.36, bf16[512,1536]{1,0:T(8,128)(2,1)} %copy-done.36, bf16[512,1536]{1,0:T(8,128)(2,1)} %copy-done.35, bf16[512,1536]{1,0:T(8,128)(2,1)} %copy-done.35, ...), custom_call_target="tpu_custom_call" | custom-call | flops 999999995904 | bytes 1000 | tf_op jit(solution)/shard_map/gradient/pallas_call | solution.py:865
  545.4 5.1 collective-permute-done.18.first.second
  554.0 3.2 finish_output.2.before
  557.3 4.5 add_convert_fusion.9
  567.9 3.1 add_convert_fusion
  574.2 17.0 %collective-permute-done.22.last = bf16[768,512]{1,0:T(8,128)(2,1)} collective-permute-done((bf16[768,512]{1,0:T(8,128)(2,1)}, bf16[768,512]{1,0:T(8,128)(2,1)}, u32[]{:S(2)}, u32[]{:S(2)}) %collective-permute-start.22) | collective-permute-done | bytes 786464 | tf_op jit(solution)/shard_map/ppermute | solution.py:1017
  591.2 5.9 input_back.3
  599.2 7.3 %gradient.9 = (bf16[768,768]{1,0:T(8,128)(2,1)}, bf16[768,768]{1,0:T(8,128)(2,1)}) custom-call(s32[4]{0:T(128)} %pad_add_fusion.1.order.before, bf16[512,1536]{1,0:T(8,128)(2,1)} %copy-done.36, bf16[512,1536]{1,0:T(8,128)(2,1)} %copy-done.36, bf16[512,1536]{1,0:T(8,128)(2,1)} %copy-done.35, bf16[512,1536]{1,0:T(8,128)(2,1)} %copy-done.35, ...), custom_call_target="tpu_custom_call" | custom-call | flops 999999995904 | bytes 1000 | tf_op jit(solution)/shard_map/gradient/pallas_call | solution.py:865
  614.1 4.2 finish_input.2.before
  621.3 3.6 collective-permute-done.25
  633.5 6.8 feed_out.3.feed
  644.0 15.5 %collective-permute-done.29 = bf16[2,96,1536]{2,1,0:T(8,128)(2,1)} collective-permute-done((bf16[2,96,1536]{2,1,0:T(8,128)(2,1)}, bf16[2,96,1536]{2,1,0:T(8,128)(2,1)}, u32[]{:S(2)}, u32[]{:S(2)}) %collective-permute-start.29) | collective-permute-done | bytes 589856 | tf_op jit(solution)/shard_map/ppermute | solution.py:1017
  661.7 4.0 finish_input.3
  665.7 5.5 collective-permute-done.31
  676.8 4.5 slice_reduce_fusion
  691.8 3.5 finish_output.3
  (386 shorter events, 142.7 us)
Async XLA Ops:
  7.2 63.6 %copy-start = (s32[8]{0:T(128)S(1)}, s32[8]{0:T(128)}, u32[]{:S(2)}) copy-start(s32[8]{0:T(128)} %param.32) | copy-start | bytes 100
  7.2 63.3 %all-gather.4.cloned.1.call-start = ((), (), s32[]{:S(2)}) async-start(), calls=%async_computation | async-start | bytes 5431296 | tf_op jit(solution)/shard_map/all_gather | solution.py:1125
  9.6 61.8 %copy-start.96 = (bf16[96,384]{1,0:T(8,128)(2,1)}, bf16[96,384]{1,0:T(8,128)(2,1)S(1)}, u32[]{:S(2)}) copy-start(bf16[96,384]{1,0:T(8,128)(2,1)S(1)} %convert_element_type.243) | copy-start | bytes 221188
  10.6 60.9 %copy-start.98 = (bf16[96,384]{1,0:T(8,128)(2,1)}, bf16[96,384]{1,0:T(8,128)(2,1)S(1)}, u32[]{:S(2)}) copy-start(bf16[96,384]{1,0:T(8,128)(2,1)S(1)} %convert_element_type.242) | copy-start | bytes 221188
  11.6 60.0 %copy-start.72 = (f32[96,2048]{1,0:T(8,128)S(1)}, f32[96,2048]{1,0:T(8,128)}, u32[]{:S(2)}) copy-start(f32[96,2048]{1,0:T(8,128)} %param.38) | copy-start | bytes 2359300
  12.4 269.2 %all-gather.6.cloned.1.call-start = ((), (), s32[]{:S(2)}) async-start(), calls=%async_computation.1 | async-start | bytes 5013504 | tf_op jit(solution)/shard_map/all_gather | solution.py:1127
  12.5 6.9 collective-permute-start.4
  70.6 248.5 %all-gather.8.cloned.1.call-start = ((), (), s32[]{:S(2)}) async-start(), calls=%async_computation.2 | async-start | bytes 20054016 | tf_op jit(solution)/shard_map/all_gather | solution.py:1163
  101.6 37.7 %collective-permute-start = (bf16[512,768]{1,0:T(8,128)(2,1)}, bf16[512,768]{1,0:T(8,128)(2,1)S(1)}, u32[]{:S(2)}, u32[]{:S(2)}) collective-permute-start(bf16[512,768]{1,0:T(8,128)(2,1)} %copy-done.12), channel_id=1, source_target_pairs={{0,1},{1,2},{2,3},{3,0},{4,5},{5,6},{6,7},{7,4},{8,9},{9,10},{10,1... | collective-permute-start | bytes 2359304 | tf_op jit(solution)/shard_map/ppermute | solution.py:1028
  103.2 55.4 %collective-permute-start.5 = (bf16[512,768]{1,0:T(8,128)(2,1)}, bf16[512,768]{1,0:T(8,128)(2,1)S(1)}, u32[]{:S(2)}, u32[]{:S(2)}) collective-permute-start(bf16[512,768]{1,0:T(8,128)(2,1)} %copy-done.19), channel_id=1, source_target_pairs={{0,1},{1,2},{2,3},{3,0},{4,5},{5,6},{6,7},{7,4},{8,9},{9,10},{10,1... | collective-permute-start | bytes 2359304 | tf_op jit(solution)/shard_map/ppermute | solution.py:1028
  139.4 112.5 %copy-start.14 = (bf16[512,768]{1,0:T(8,128)(2,1)}, bf16[512,768]{1,0:T(8,128)(2,1)S(1)}, u32[]{:S(2)}) copy-start(bf16[512,768]{1,0:T(8,128)(2,1)S(1)} %collective-permute-done.refs_1_) | copy-start | bytes 2359300
  139.4 44.5 %collective-permute-start.1 = (bf16[512,768]{1,0:T(8,128)(2,1)S(1)}, bf16[512,768]{1,0:T(8,128)(2,1)S(1)}, u32[]{:S(2)}, u32[]{:S(2)}) collective-permute-start(bf16[512,768]{1,0:T(8,128)(2,1)S(1)} %collective-permute-done.refs_1_), channel_id=1, source_target_pairs={{0,1},{1,2},{2,3},{3,0},{4,5},{5,6},{6,7},{7,4},{8,9},{9,10},{10,1... | collective-permute-start | bytes 2359304 | tf_op jit(solution)/shard_map/ppermute | solution.py:1028
  158.6 100.9 %copy-start.21 = (bf16[512,768]{1,0:T(8,128)(2,1)}, bf16[512,768]{1,0:T(8,128)(2,1)S(1)}, u32[]{:S(2)}) copy-start(bf16[512,768]{1,0:T(8,128)(2,1)S(1)} %collective-permute-done.5.refs_1_) | copy-start | bytes 2359300
  158.6 50.6 %collective-permute-start.6 = (bf16[512,768]{1,0:T(8,128)(2,1)S(1)}, bf16[512,768]{1,0:T(8,128)(2,1)S(1)}, u32[]{:S(2)}, u32[]{:S(2)}) collective-permute-start(bf16[512,768]{1,0:T(8,128)(2,1)S(1)} %collective-permute-done.5.refs_1_), channel_id=1, source_target_pairs={{0,1},{1,2},{2,3},{3,0},{4,5},{5,6},{6,7},{7,4},{8,9},{9,10},{10,1... | collective-permute-start | bytes 2359304 | tf_op jit(solution)/shard_map/ppermute | solution.py:1028
  183.8 68.0 %copy-start.15 = (bf16[512,768]{1,0:T(8,128)(2,1)}, bf16[512,768]{1,0:T(8,128)(2,1)S(1)}, u32[]{:S(2)}) copy-start(bf16[512,768]{1,0:T(8,128)(2,1)S(1)} %collective-permute-done.1.refs_2_) | copy-start | bytes 2359300
  183.8 50.6 %collective-permute-start.2 = (bf16[512,768]{1,0:T(8,128)(2,1)S(1)}, bf16[512,768]{1,0:T(8,128)(2,1)S(1)}, u32[]{:S(2)}, u32[]{:S(2)}) collective-permute-start(bf16[512,768]{1,0:T(8,128)(2,1)S(1)} %collective-permute-done.1.refs_2_), channel_id=1, source_target_pairs={{0,1},{1,2},{2,3},{3,0},{4,5},{5,6},{6,7},{7,4},{8,9},{9,10},{10,1... | collective-permute-start | bytes 2359304 | tf_op jit(solution)/shard_map/ppermute | solution.py:1028
  209.1 50.3 %copy-start.22 = (bf16[512,768]{1,0:T(8,128)(2,1)}, bf16[512,768]{1,0:T(8,128)(2,1)S(1)}, u32[]{:S(2)}) copy-start(bf16[512,768]{1,0:T(8,128)(2,1)S(1)} %collective-permute-done.6.refs_2_) | copy-start | bytes 2359300
  209.1 50.3 %collective-permute-start.7 = (bf16[512,768]{1,0:T(8,128)(2,1)S(1)}, bf16[512,768]{1,0:T(8,128)(2,1)S(1)}, u32[]{:S(2)}, u32[]{:S(2)}) collective-permute-start(bf16[512,768]{1,0:T(8,128)(2,1)S(1)} %collective-permute-done.6.refs_2_), channel_id=1, source_target_pairs={{0,1},{1,2},{2,3},{3,0},{4,5},{5,6},{6,7},{7,4},{8,9},{9,10},{10,1... | collective-permute-start | bytes 2359304 | tf_op jit(solution)/shard_map/ppermute | solution.py:1028
  209.2 50.3 %copy-start.30 = (s32[10]{0:T(128)}, s32[10]{0:T(128)S(1)}, u32[]{:S(2)}) copy-start(s32[10]{0:T(128)S(1)} %pad_add_fusion.spans) | copy-start | bytes 124
  252.7 28.9 %collective-permute-start.3 = (bf16[512,768]{1,0:T(8,128)(2,1)}, bf16[512,768]{1,0:T(8,128)(2,1)}, u32[]{:S(2)}, u32[]{:S(2)}) collective-permute-start(bf16[512,768]{1,0:T(8,128)(2,1)} %get-tuple-element.139.own.refs_5_), channel_id=1, source_target_pairs={{0,16},{16,0},{1,17},{17,1},{2,18},{18,2},{3,19},{19,3},{4,20},{20... | collective-permute-start | bytes 2359304 | tf_op jit(solution)/shard_map/ppermute | solution.py:1017
  275.8 19.4 %collective-permute-start.8 = (bf16[512,768]{1,0:T(8,128)(2,1)}, bf16[512,768]{1,0:T(8,128)(2,1)}, u32[]{:S(2)}, u32[]{:S(2)}) collective-permute-start(bf16[512,768]{1,0:T(8,128)(2,1)} %get-tuple-element.145.own.refs_4_), channel_id=1, source_target_pairs={{0,16},{16,0},{1,17},{17,1},{2,18},{18,2},{3,19},{19,3},{4,20},{20... | collective-permute-start | bytes 2359304 | tf_op jit(solution)/shard_map/ppermute | solution.py:1017
  346.3 42.4 %collective-permute-start.9 = (bf16[512,1536]{1,0:T(8,128)(2,1)}, bf16[512,1536]{1,0:T(8,128)(2,1)}, u32[]{:S(2)}, u32[]{:S(2)}) collective-permute-start(bf16[512,1536]{1,0:T(8,128)(2,1)} %copy_out.6), channel_id=1, source_target_pairs={{0,16},{16,0},{1,17},{17,1},{2,18},{18,2},{3,19},{19,3},{4,20},{20... | collective-permute-start | bytes 4718600 | tf_op jit(solution)/shard_map/ppermute | solution.py:1017
  374.8 72.4 %collective-permute-start.10 = (bf16[512,1536]{1,0:T(8,128)(2,1)}, bf16[512,1536]{1,0:T(8,128)(2,1)}, u32[]{:S(2)}, u32[]{:S(2)}) collective-permute-start(bf16[512,1536]{1,0:T(8,128)(2,1)} %copy_out.7), channel_id=1, source_target_pairs={{0,16},{16,0},{1,17},{17,1},{2,18},{18,2},{3,19},{19,3},{4,20},{20... | collective-permute-start | bytes 4718600 | tf_op jit(solution)/shard_map/ppermute | solution.py:1017
  388.7 6.5 collective-permute-start.11
  402.2 67.5 %collective-permute-start.14 = (bf16[384,2048]{1,0:T(8,128)(2,1)}, bf16[384,2048]{1,0:T(8,128)(2,1)}, u32[]{:S(2)}, u32[]{:S(2)}) collective-permute-start(bf16[384,2048]{1,0:T(8,128)(2,1)} %get-tuple-element.351), channel_id=1, source_target_pairs={{0,8},{4,12},{8,0},{12,4},{1,9},{5,13},{9,1},{13,5},{2,10},{6,14},... | collective-permute-start | bytes 4718600 | tf_op jit(solution)/shard_map/ppermute | solution.py:1017
  425.0 40.7 %collective-permute-start.13 = (bf16[2,768,512]{2,1,0:T(8,128)(2,1)}, bf16[2,768,512]{2,1,0:T(8,128)(2,1)}, u32[]{:S(2)}, u32[]{:S(2)}) collective-permute-start(bf16[2,768,512]{2,1,0:T(8,128)(2,1)} %copy_out.8), channel_id=1, source_target_pairs={{0,1},{1,0},{2,3},{3,2},{4,5},{5,4},{6,7},{7,6},{8,9},{9,8},{10,11... | collective-permute-start | bytes 4718600 | tf_op jit(solution)/shard_map/ppermute | solution.py:1017
  447.2 10.6 %collective-permute-start.12 = (bf16[768,4096]{1,0:T(8,128)(2,1)}, bf16[768,4096]{1,0:T(8,128)(2,1)}, u32[]{:S(2)}, u32[]{:S(2)}) collective-permute-start(bf16[768,4096]{1,0:T(8,128)(2,1)} %get-tuple-element.181), channel_id=1, source_target_pairs={{0,4},{4,0},{8,12},{12,8},{1,5},{5,1},{9,13},{13,9},{2,6},{6,2},{1... | collective-permute-start | bytes 18874376 | tf_op jit(solution)/shard_map/ppermute | solution.py:1017
  468.4 44.7 %collective-permute-start.16 = (bf16[768,512]{1,0:T(8,128)(2,1)}, bf16[768,512]{1,0:T(8,128)(2,1)}, u32[]{:S(2)}, u32[]{:S(2)}) collective-permute-start(bf16[768,512]{1,0:T(8,128)(2,1)} %fusion.3), channel_id=1, source_target_pairs={{0,2},{1,3},{2,0},{3,1},{4,6},{5,7},{6,4},{7,5},{8,10},{9,11},{10,... | collective-permute-start | bytes 2359304 | tf_op jit(solution)/shard_map/ppermute | solution.py:1017
  472.9 36.6 %collective-permute-start.15 = (bf16[2,96,2048]{2,1,0:T(8,128)(2,1)}, bf16[2,96,2048]{2,1,0:T(8,128)(2,1)}, u32[]{:S(2)}, u32[]{:S(2)}) collective-permute-start(bf16[2,96,2048]{2,1,0:T(8,128)(2,1)} %get-tuple-element.367), channel_id=1, source_target_pairs={{0,1},{1,0},{2,3},{3,2},{4,5},{5,4},{6,7},{7,6},{8,9},{9,8},{10,11... | collective-permute-start | bytes 2359304 | tf_op jit(solution)/shard_map/ppermute | solution.py:1017
  495.8 54.8 %collective-permute-start.18 = (bf16[2,768,512]{2,1,0:T(8,128)(2,1)}, bf16[2,768,512]{2,1,0:T(8,128)(2,1)}, u32[]{:S(2)}, u32[]{:S(2)}) collective-permute-start(bf16[2,768,512]{2,1,0:T(8,128)(2,1)} %copy_out.9), channel_id=1, source_target_pairs={{0,1},{1,0},{2,3},{3,2},{4,5},{5,4},{6,7},{7,6},{8,9},{9,8},{10,11... | collective-permute-start | bytes 4718600 | tf_op jit(solution)/shard_map/ppermute | solution.py:1017
  497.0 71.0 %collective-permute-start.21 = (bf16[384,4096]{1,0:T(8,128)(2,1)}, bf16[384,4096]{1,0:T(8,128)(2,1)}, u32[]{:S(2)}, u32[]{:S(2)}) collective-permute-start(bf16[384,4096]{1,0:T(8,128)(2,1)} %get-tuple-element.349), channel_id=1, source_target_pairs={{0,8},{4,12},{8,0},{12,4},{1,9},{5,13},{9,1},{13,5},{2,10},{6,14},... | collective-permute-start | bytes 9437192 | tf_op jit(solution)/shard_map/ppermute | solution.py:1017
  505.6 47.5 %collective-permute-start.17 = (bf16[512,1536]{1,0:T(8,128)(2,1)}, bf16[512,1536]{1,0:T(8,128)(2,1)}, u32[]{:S(2)}, u32[]{:S(2)}) collective-permute-start(bf16[512,1536]{1,0:T(8,128)(2,1)} %feed_out.2.feed), channel_id=1, source_target_pairs={{0,16},{16,0},{1,17},{17,1},{2,18},{18,2},{3,19},{19,3},{4,20},{20... | collective-permute-start | bytes 4718600 | tf_op jit(solution)/shard_map/ppermute | solution.py:1017
  511.9 51.9 %collective-permute-start.20 = (bf16[96,2048]{1,0:T(8,128)(2,1)}, bf16[96,2048]{1,0:T(8,128)(2,1)}, u32[]{:S(2)}, u32[]{:S(2)}) collective-permute-start(bf16[96,2048]{1,0:T(8,128)(2,1)} %get-tuple-element.371), channel_id=1, source_target_pairs={{0,2},{1,3},{2,0},{3,1},{4,6},{5,7},{6,4},{7,5},{8,10},{9,11},{10,... | collective-permute-start | bytes 1179656 | tf_op jit(solution)/shard_map/ppermute | solution.py:1017
  524.2 86.6 %collective-permute-start.23 = (bf16[512,1536]{1,0:T(8,128)(2,1)}, bf16[512,1536]{1,0:T(8,128)(2,1)}, u32[]{:S(2)}, u32[]{:S(2)}) collective-permute-start(bf16[512,1536]{1,0:T(8,128)(2,1)} %copy_out.10), channel_id=1, source_target_pairs={{0,16},{16,0},{1,17},{17,1},{2,18},{18,2},{3,19},{19,3},{4,20},{20... | collective-permute-start | bytes 4718600 | tf_op jit(solution)/shard_map/ppermute | solution.py:1017
  550.5 6.7 collective-permute-start.19
  553.1 38.1 %collective-permute-start.22 = (bf16[768,512]{1,0:T(8,128)(2,1)}, bf16[768,512]{1,0:T(8,128)(2,1)}, u32[]{:S(2)}, u32[]{:S(2)}) collective-permute-start(bf16[768,512]{1,0:T(8,128)(2,1)} %fusion.4), channel_id=1, source_target_pairs={{0,2},{1,3},{2,0},{3,1},{4,6},{5,7},{6,4},{7,5},{8,10},{9,11},{10,... | collective-permute-start | bytes 2359304 | tf_op jit(solution)/shard_map/ppermute | solution.py:1017
  561.8 66.3 %collective-permute-start.26 = (bf16[384,1536]{1,0:T(8,128)(2,1)}, bf16[384,1536]{1,0:T(8,128)(2,1)}, u32[]{:S(2)}, u32[]{:S(2)}) collective-permute-start(bf16[384,1536]{1,0:T(8,128)(2,1)} %get-tuple-element.353), channel_id=1, source_target_pairs={{0,8},{4,12},{8,0},{12,4},{1,9},{5,13},{9,1},{13,5},{2,10},{6,14},... | collective-permute-start | bytes 3538952 | tf_op jit(solution)/shard_map/ppermute | solution.py:1017
  572.9 51.9 %collective-permute-start.25 = (bf16[2,96,4096]{2,1,0:T(8,128)(2,1)}, bf16[2,96,4096]{2,1,0:T(8,128)(2,1)}, u32[]{:S(2)}, u32[]{:S(2)}) collective-permute-start(bf16[2,96,4096]{2,1,0:T(8,128)(2,1)} %get-tuple-element.355), channel_id=1, source_target_pairs={{0,1},{1,0},{2,3},{3,2},{4,5},{5,4},{6,7},{7,6},{8,9},{9,8},{10,11... | collective-permute-start | bytes 4718600 | tf_op jit(solution)/shard_map/ppermute | solution.py:1017
  606.5 11.8 %collective-permute-start.24 = (bf16[768,768]{1,0:T(8,128)(2,1)}, bf16[768,768]{1,0:T(8,128)(2,1)}, u32[]{:S(2)}, u32[]{:S(2)}) collective-permute-start(bf16[768,768]{1,0:T(8,128)(2,1)} %get-tuple-element.224), channel_id=1, source_target_pairs={{0,4},{4,0},{8,12},{12,8},{1,5},{5,1},{9,13},{13,9},{2,6},{6,2},{1... | collective-permute-start | bytes 3538952 | tf_op jit(solution)/shard_map/ppermute | solution.py:1017
  609.3 52.4 %collective-permute-start.30 = (bf16[512,1536]{1,0:T(8,128)(2,1)}, bf16[512,1536]{1,0:T(8,128)(2,1)}, u32[]{:S(2)}, u32[]{:S(2)}) collective-permute-start(bf16[512,1536]{1,0:T(8,128)(2,1)} %copy_out.11), channel_id=1, source_target_pairs={{0,16},{16,0},{1,17},{17,1},{2,18},{18,2},{3,19},{19,3},{4,20},{20... | collective-permute-start | bytes 4718600 | tf_op jit(solution)/shard_map/ppermute | solution.py:1017
  620.9 20.9 %collective-permute-start.28 = (bf16[384,768]{1,0:T(8,128)(2,1)}, bf16[384,768]{1,0:T(8,128)(2,1)}, u32[]{:S(2)}, u32[]{:S(2)}) collective-permute-start(bf16[384,768]{1,0:T(8,128)(2,1)} %get-tuple-element.361), channel_id=1, source_target_pairs={{0,8},{4,12},{8,0},{12,4},{1,9},{5,13},{9,1},{13,5},{2,10},{6,14},... | collective-permute-start | bytes 1769480 | tf_op jit(solution)/shard_map/ppermute | solution.py:1017
  631.1 28.3 %collective-permute-start.29 = (bf16[2,96,1536]{2,1,0:T(8,128)(2,1)}, bf16[2,96,1536]{2,1,0:T(8,128)(2,1)}, u32[]{:S(2)}, u32[]{:S(2)}) collective-permute-start(bf16[2,96,1536]{2,1,0:T(8,128)(2,1)} %get-tuple-element.369), channel_id=1, source_target_pairs={{0,1},{1,0},{2,3},{3,2},{4,5},{5,4},{6,7},{7,6},{8,9},{9,8},{10,11... | collective-permute-start | bytes 1769480 | tf_op jit(solution)/shard_map/ppermute | solution.py:1017
  631.1 42.0 %collective-permute-start.32 = (bf16[96,4096]{1,0:T(8,128)(2,1)}, bf16[96,4096]{1,0:T(8,128)(2,1)}, u32[]{:S(2)}, u32[]{:S(2)}) collective-permute-start(bf16[96,4096]{1,0:T(8,128)(2,1)} %get-tuple-element.365), channel_id=1, source_target_pairs={{0,2},{1,3},{2,0},{3,1},{4,6},{5,7},{6,4},{7,5},{8,10},{9,11},{10,... | collective-permute-start | bytes 2359304 | tf_op jit(solution)/shard_map/ppermute | solution.py:1017
  640.3 51.3 %collective-permute-start.27 = (bf16[512,1536]{1,0:T(8,128)(2,1)}, bf16[512,1536]{1,0:T(8,128)(2,1)}, u32[]{:S(2)}, u32[]{:S(2)}) collective-permute-start(bf16[512,1536]{1,0:T(8,128)(2,1)} %feed_out.3.feed), channel_id=1, source_target_pairs={{0,16},{16,0},{1,17},{17,1},{2,18},{18,2},{3,19},{19,3},{4,20},{20... | collective-permute-start | bytes 4718600 | tf_op jit(solution)/shard_map/ppermute | solution.py:1017
  644.0 27.2 %collective-permute-start.31 = (bf16[2,96,768]{2,1,0:T(8,128)(2,1)}, bf16[2,96,768]{2,1,0:T(8,128)(2,1)}, u32[]{:S(2)}, u32[]{:S(2)}) collective-permute-start(bf16[2,96,768]{2,1,0:T(8,128)(2,1)} %get-tuple-element.373), channel_id=1, source_target_pairs={{0,1},{1,0},{2,3},{3,2},{4,5},{5,4},{6,7},{7,6},{8,9},{9,8},{10,11... | collective-permute-start | bytes 884744 | tf_op jit(solution)/shard_map/ppermute | solution.py:1017
  661.5 26.1 %collective-permute-start.33 = (bf16[96,1536]{1,0:T(8,128)(2,1)}, bf16[96,1536]{1,0:T(8,128)(2,1)}, u32[]{:S(2)}, u32[]{:S(2)}) collective-permute-start(bf16[96,1536]{1,0:T(8,128)(2,1)} %get-tuple-element.375), channel_id=1, source_target_pairs={{0,2},{1,3},{2,0},{3,1},{4,6},{5,7},{6,4},{7,5},{8,10},{9,11},{10,... | collective-permute-start | bytes 884744 | tf_op jit(solution)/shard_map/ppermute | solution.py:1017
  673.0 22.4 %collective-permute-start.34 = (bf16[96,768]{1,0:T(8,128)(2,1)}, bf16[96,768]{1,0:T(8,128)(2,1)}, u32[]{:S(2)}, u32[]{:S(2)}) collective-permute-start(bf16[96,768]{1,0:T(8,128)(2,1)} %get-tuple-element.383), channel_id=1, source_target_pairs={{0,2},{1,3},{2,0},{3,1},{4,6},{5,7},{6,4},{7,5},{8,10},{9,11},{10,... | collective-permute-start | bytes 442376 | tf_op jit(solution)/shard_map/ppermute | solution.py:1017
  696.5 3.6 collective-permute-start.35
  (114 other events, 744.6 us)
Sparse Core Ops, SparseCore 0:
  12.5 57.9 all-gather.3
  73.4 62.7 all-gather.5
  138.4 180.6 all-gather.7
